TPU v7x, 32 devices: a whole 2x2x4 slice. The times are simulated.
32 devices in a mesh: lat: 8 (over z, y), lon: 4 (over x, core).
Axes of the slice: x: 2, y: 2, z: 4, core: 2. Of those that a mesh axis runs over, the one named last changes fastest.
Arguments:
- field: bfloat16 [64, 1440, 256], P('lat', 'lon'), may hold values from -6 to 6
- cotangent: bfloat16 [64, 1440, 256], P('lat', 'lon'), may hold values from -0.118585412 to 0.118585412
- legendre: bfloat16 [384, 64, 384], P('lat'), may hold values from -0.75 to 0.75
- quad_weight: float32 [64], P('lat'), may hold values from 0.25 to 2
- order_slots: int32 [384], replicated, may hold values from 0 to 383, as said below
- support_blocks: int32 [8, 3], P('lat'), may hold values from 0 to 7, as said below
- filter_values: bfloat16 [3, 64, 3, 8], P(None, 'lat'), may hold values from -1.25 to 1.25
- spectral_weight: bfloat16 [2, 256, 256], replicated, may hold values from -0.25 to 0.25
- disco_weight: bfloat16 [3, 256, 256], replicated, may hold values from -0.21875 to 0.21875
Outputs:
- output: bfloat16 [64, 1440, 256], P('lat', 'lon')
- grad_spectral: float32 [2, 256, 256], replicated
- grad_disco: float32 [3, 256, 256], replicated
Inputs may be any that keep to these rules, and one draw needn't show every extreme that they name: order_slots holds every order from 0 to 383 exactly once; the first slot of each block of 384 // 8 slots holds an order below 8. `support_blocks`: slot 0 of row block b names b itself; slots 1 and 2 name b - 1, b or b + 1.
All inputs are finite; a program needn't handle non-finite values.
Results may differ from a plain program's by a relative error of at most 0.015.
Values may be sent and summed in bfloat16 or wider, within the bound.
A program may use at most 128 MiB of HBM per device.

v0:
```python
import jax
import jax.numpy as jnp
from jax import lax
from jax.sharding import PartitionSpec as P


def padded(value, sides, width, wrap):
    for axis, dim in sides:
        size, length = (lax.axis_size(axis), value.shape[dim])
        up = [(i, (i + 1) % size) for i in range(size if wrap else size - 1)]
        down = [(j, i) for i, j in up]
        last = lax.slice_in_dim(value, length - width, length, axis=dim)
        leading = lax.slice_in_dim(value, 0, width, axis=dim)
        before = lax.ppermute(last, axis, up)
        after = lax.ppermute(leading, axis, down)
        value = jnp.concatenate([before, value, after], axis=dim)
    return value


def fourier_tables(order_slots, nlon):
    column = jnp.arange(nlon, dtype=jnp.int32)
    phase = column[:, None] * order_slots[None, :] % nlon
    angle = phase.astype(jnp.float32) * (2.0 * jnp.pi / nlon)
    cosine = jnp.cos(angle)
    sine = jnp.sin(angle)
    factor = jnp.where(order_slots == 0, 1.0, 2.0).astype(jnp.float32)[None, :]
    analysis_table = jnp.concatenate([cosine / nlon, -sine / nlon], axis=1).astype(jnp.bfloat16)
    synthesis_table = jnp.concatenate([factor * cosine, -factor * sine], axis=1).astype(
        jnp.bfloat16
    )
    return (analysis_table, synthesis_table)


def outer_sum(left, right):
    return lax.dot_general(
        left, right, (((0,), (0,)), ((), ())), preferred_element_type=jnp.float32
    )


def complex_mix(real_part, imag_part, w_real, w_imag):
    out_real = jnp.dot(real_part, w_real, preferred_element_type=jnp.float32) - jnp.dot(
        imag_part, w_imag, preferred_element_type=jnp.float32
    )
    out_imag = jnp.dot(real_part, w_imag, preferred_element_type=jnp.float32) + jnp.dot(
        imag_part, w_real, preferred_element_type=jnp.float32
    )
    return (out_real, out_imag)


def to_degrees(values):
    return lax.all_to_all(values, "lon", split_axis=1, concat_axis=3, tiled=True)


def local(
    field,
    cotangent,
    legendre,
    quad_weight,
    order_slots,
    support_blocks,
    filter_values,
    spectral_weight,
    disco_weight,
):
    f32 = jnp.float32
    bf16 = jnp.bfloat16
    lat_rows, lon_cols, channels = field.shape
    nlon = lon_cols * lax.axis_size("lon")
    slots_dev, nlat, degrees = legendre.shape
    quarter = channels // lax.axis_size("lon")
    mmax = order_slots.shape[0]
    lat_pos = lax.axis_index("lat")
    analysis_table, synthesis_table = fourier_tables(order_slots, nlon)
    own_orders = lax.dynamic_slice_in_dim(order_slots, lat_pos * slots_dev, slots_dev)
    degree_mask = (jnp.arange(degrees, dtype=jnp.int32)[None, :] >= own_orders[:, None]).astype(f32)

    def longitude_transform(values, table):
        slabs = lax.all_to_all(values, "lon", split_axis=2, concat_axis=1, tiled=True)
        return jnp.einsum("ajc,jq->aqc", slabs, table, preferred_element_type=f32)

    def legendre_forward(spectrum):
        shaped = spectrum.reshape(lat_rows, 2, mmax, -1).astype(bf16)
        coeffs = jnp.einsum(
            "kal,arkc->klrc",
            legendre,
            lax.all_to_all(shaped, "lat", split_axis=2, concat_axis=0, tiled=True),
            preferred_element_type=f32,
        )
        return (coeffs * degree_mask[:, :, None, None]).astype(bf16)

    spectrum = longitude_transform(field, analysis_table) * quad_weight[:, None, None]
    coeffs = legendre_forward(spectrum)
    degree_coeffs = to_degrees(coeffs)
    real_part = degree_coeffs[:, :, 0].reshape(-1, channels)
    imag_part = degree_coeffs[:, :, 1].reshape(-1, channels)
    out_real, out_imag = complex_mix(real_part, imag_part, spectral_weight[0], spectral_weight[1])
    mixed_degrees = jnp.stack(
        [out_real.reshape(slots_dev, -1, channels), out_imag.reshape(slots_dev, -1, channels)],
        axis=2,
    ).astype(bf16)
    mixed = lax.all_to_all(mixed_degrees, "lon", split_axis=3, concat_axis=1, tiled=True)
    masked = mixed * degree_mask.astype(bf16)[:, :, None, None]
    grid_spectrum = jnp.einsum(
        "kal,klrc->arkc", legendre, masked, preferred_element_type=f32
    ).astype(bf16)
    lat_spectrum = lax.all_to_all(grid_spectrum, "lat", split_axis=0, concat_axis=2, tiled=True)
    partial_field = jnp.einsum(
        "aqc,jq->ajc",
        lat_spectrum.reshape(lat_rows, 2 * mmax, quarter),
        synthesis_table,
        preferred_element_type=f32,
    ).astype(bf16)
    spectral_out = lax.all_to_all(partial_field, "lon", split_axis=1, concat_axis=2, tiled=True)
    rimmed = padded(field, (("lon", 1),), 1, True)
    extended = padded(rimmed, (("lat", 0),), lat_rows, False)
    picks = support_blocks[0] - lat_pos + 1
    onehot = (picks[:, None] == jnp.arange(3, dtype=jnp.int32)[None, :]).astype(f32)
    operator = (
        jnp.einsum("tasb,sq->taqb", filter_values.astype(f32), onehot)
        .reshape(3, lat_rows, 3 * lat_rows)
        .astype(bf16)
    )
    responses = []
    disco_sum = jnp.zeros((lat_rows * lon_cols, channels), f32)
    for tap in range(3):
        window = extended[:, tap : tap + lon_cols]
        response = jnp.einsum(
            "ab,boc->aoc", operator[tap], window, preferred_element_type=f32
        ).astype(bf16)
        responses.append(response)
        disco_sum = disco_sum + jnp.dot(
            response.reshape(-1, channels), disco_weight[tap], preferred_element_type=f32
        )
    pre_act = spectral_out.astype(f32) + disco_sum.reshape(lat_rows, lon_cols, channels)
    activated, pullback = jax.vjp(jax.nn.gelu, pre_act)
    output = (field.astype(f32) + activated).astype(bf16)
    (grad_pre,) = pullback(cotangent.astype(f32))
    grad_pre = grad_pre.astype(bf16)
    flat_grad = grad_pre.reshape(-1, channels)
    disco_terms = jnp.stack(
        [outer_sum(response.reshape(-1, channels), flat_grad) for response in responses]
    )
    grad_disco = lax.psum(disco_terms, ("lat", "lon"))
    grad_grid = longitude_transform(grad_pre, synthesis_table)
    grad_coeffs = legendre_forward(grad_grid)
    degree_grad = to_degrees(grad_coeffs)
    grad_real = degree_grad[:, :, 0].reshape(-1, channels)
    grad_imag = degree_grad[:, :, 1].reshape(-1, channels)
    g_real = outer_sum(real_part, grad_real) + outer_sum(imag_part, grad_imag)
    g_imag = outer_sum(real_part, grad_imag) - outer_sum(imag_part, grad_real)
    grad_spectral = lax.psum(jnp.stack([g_real, g_imag]), ("lat", "lon"))
    return (output, grad_spectral, grad_disco)


def solution(mesh):
    placed = (
        P("lat", "lon", None),
        P("lat", "lon", None),
        P("lat", None, None),
        P("lat"),
        P(),
        P("lat", None),
        P(None, "lat", None, None),
        P(),
        P(),
    )
    return jax.shard_map(
        local,
        mesh=mesh,
        in_specs=placed,
        out_specs=(P("lat", "lon", None), P(), P()),
        check_vma=False,
    )
```

profile of v0, /device:TPU:25, one launch (start us, length us, event | category | flops | bytes accessed | tf_op | source)
XLA Modules:
  0.0 870.8 jit_solution(12715716816381791071)
XLA Ops:
  15.2 11.3 %multiply_convert_fusion.5 = (bf16[1440,384]{1,0:T(8,128)(2,1)}, bf16[1440,384]{1,0:T(8,128)(2,1)S(1)}, bf16[1440,384]{1,0:T(8,128)(2,1)}, bf16[1440,384]{1,0:T(8,128)(2,1)}) fusion(s32[384]{0:T(512)S(1)} %copy-done.14, f32[384]{0:T(512)S(1)} %get-tuple-element.27, f32[384]{0:T(512)S(1)} %get-tuple-element.28), kind=kLoop, calls=%fused_computation.60 | loop fusion | flops 9953280 | bytes 4428288 | tf_op jit(solution)/shard_map/convert.9
  26.5 8.0 all-to-all-done
  54.7 5.5 all-to-all-start.1
  60.4 17.5 %all-to-all-done.1 = bf16[8,2,24576]{2,1,0:T(2,128)(2,1)S(1)} async-done(((bf16[8,2,24576]{2,1,0:T(2,128)(2,1)}), bf16[8,2,24576]{2,1,0:T(2,128)(2,1)S(1)}, u32[]{:S(2)}, u32[]{:S(2)}) %all-to-all-start.1) | async-done | bytes 786464 | tf_op jit(solution)/shard_map/all_to_all | solution.py:86
  84.9 20.4 %copy.152 = bf16[48,384,2,64]{3,2,0,1:T(2,128)(2,1)} copy(bf16[48,384,2,64]{1,3,2,0:T(8,128)(2,1)} %fusion.2) | data formatting | bytes 9437184 | tf_op jit(solution)/shard_map/convert_element_type | solution.py:89
  105.2 10.4 %reshape.147 = bf16[4,2,294912]{2,1,0:T(2,128)(2,1)} reshape(bf16[384,48,2,64]{3,2,1,0:T(2,128)(2,1)} %bitcast.243) | data formatting | bytes 9437184
  115.6 60.0 %all_to_all.150 = bf16[4,2,294912]{2,1,0:T(2,128)(2,1)} all-to-all(bf16[4,2,294912]{2,1,0:T(2,128)(2,1)} %reshape.147), channel_id=1, replica_groups=mesh['lat'=8,'lon'=4] {'lon'}, dimensions={0} | all-to-all | bytes 9437184 | tf_op jit(solution)/shard_map/all_to_all | solution.py:51
  175.5 10.2 %reshape.148 = bf16[384,48,2,64]{3,2,1,0:T(2,128)(2,1)} reshape(bf16[4,2,294912]{2,1,0:T(2,128)(2,1)} %all_to_all.150) | data formatting | bytes 9437184
  185.7 21.4 %copy.153 = bf16[48,4,96,2,64]{2,4,1,3,0:T(8,128)(2,1)} copy(bf16[48,4,96,2,64]{4,3,0,2,1:T(2,128)(2,1)} %bitcast.244) | data formatting | bytes 9437184 | tf_op jit(solution)/shard_map/all_to_all | solution.py:51
  207.1 6.3 fusion.130
  230.1 5.3 fusion
  235.4 13.8 %copy.156 = bf16[48,96,1,256]{1,2,0,3:T(2,128)(2,1)} copy(bf16[48,96,1,256]{3,1,0,2:T(8,128)(2,1)} %bitcast.264) | data formatting | bytes 4718592 | tf_op jit(solution)/shard_map/stack;reshape | solution.py:97
  254.4 13.9 %copy.157 = bf16[48,96,1,256]{1,2,0,3:T(2,128)(2,1)} copy(bf16[48,96,1,256]{3,1,0,2:T(8,128)(2,1)} %bitcast.263) | data formatting | bytes 4718592 | tf_op jit(solution)/shard_map/stack;reshape | solution.py:97
  268.4 19.2 %pad_maximum_fusion = bf16[48,96,2,256]{1,2,0,3:T(2,128)(2,1)} fusion(bf16[48,96,1,256]{1,2,0,3:T(2,128)(2,1)} %copy.157, bf16[48,96,1,256]{1,2,0,3:T(2,128)(2,1)} %copy.156), kind=kLoop, calls=%fused_computation.6 | loop fusion | flops 9437184 | bytes 9437184 | tf_op jit(solution)/shard_map/stack | solution.py:97
  287.6 6.2 all-to-all-start.3
  296.3 65.5 %collective-permute-done = bf16[8,1,256]{2,0,1:T(8,128)(2,1)S(1)} collective-permute-done((bf16[8,1,256]{2,0,1:T(8,128)(2,1)S(1)}, bf16[8,1,256]{2,0,1:T(8,128)(2,1)S(1)}, u32[]{:S(2)}, u32[]{:S(2)}) %collective-permute-start) | collective-permute-done | bytes 4128 | tf_op jit(solution)/shard_map/ppermute | solution.py:14
  372.7 7.9 copy.158
  380.6 18.3 %copy.159 = bf16[48,4,96,2,64]{2,1,4,3,0:T(4,128)(2,1)} copy(bf16[48,4,96,2,64]{2,4,1,3,0:T(8,128)(2,1)} %bitcast.249) | data formatting | bytes 9437184 | tf_op jit(solution)/shard_map/all_to_all | solution.py:101
  398.9 10.8 %all_to_all.124 = bf16[48,384,2,64]{1,3,2,0:T(8,128)(2,1)} reshape(bf16[48,4,96,2,64]{2,1,4,3,0:T(4,128)(2,1)} %copy.159) | data formatting | bytes 9437184 | tf_op jit(solution)/shard_map/all_to_all | solution.py:101
  422.8 6.5 all-to-all-start.4
  429.3 9.1 %collective-permute-done.3 = bf16[8,362,256]{2,0,1:T(8,128)(2,1)} collective-permute-done((bf16[8,362,256]{2,0,1:T(8,128)(2,1)}, bf16[8,362,256]{2,0,1:T(8,128)(2,1)}, u32[]{:S(2)}, u32[]{:S(2)}) %collective-permute-start.3) | collective-permute-done | bytes 1482784 | tf_op jit(solution)/shard_map/ppermute | solution.py:15
  487.8 12.6 %all-to-all-done.5 = bf16[4,2,92160]{2,1,0:T(2,128)(2,1)} async-done(((bf16[4,2,92160]{2,1,0:T(2,128)(2,1)}), bf16[4,2,92160]{2,1,0:T(2,128)(2,1)}, u32[]{:S(2)}, u32[]{:S(2)}) %all-to-all-start.5) | async-done | bytes 1474592 | tf_op jit(solution)/shard_map/all_to_all | solution.py:113
  514.1 5.9 fusion.22
  522.9 23.5 %all_to_all.151 = bf16[8,360,256]{1,0,2:T(8,128)(2,1)S(1)} all-to-all(bf16[8,360,256]{1,0,2:T(8,128)(2,1)} %copy.173), channel_id=1, replica_groups=mesh['lat'=8,'lon'=4] {'lon'}, dimensions={2} | all-to-all | bytes 2949120 | tf_op jit(solution)/shard_map/all_to_all | solution.py:78
  564.3 24.1 %all_to_all.152 = bf16[8,2,24576]{2,1,0:T(2,128)(2,1)} all-to-all(bf16[8,2,24576]{2,1,0:T(2,128)(2,1)S(1)} %reshape.153), channel_id=1, replica_groups=mesh['lat'=8,'lon'=4] {'lat'}, dimensions={0} | all-to-all | bytes 1572864 | tf_op jit(solution)/shard_map/all_to_all | solution.py:86
  596.4 20.4 %copy.180 = bf16[48,384,2,64]{3,2,0,1:T(2,128)(2,1)} copy(bf16[48,384,2,64]{1,3,2,0:T(8,128)(2,1)} %fusion.3) | data formatting | bytes 9437184 | tf_op jit(solution)/shard_map/convert_element_type | solution.py:89
  616.8 10.5 %reshape.155 = bf16[4,2,294912]{2,1,0:T(2,128)(2,1)} reshape(bf16[384,48,2,64]{3,2,1,0:T(2,128)(2,1)} %bitcast.245) | data formatting | bytes 9437184
  627.3 6.4 all-to-all-start.8
  639.4 47.2 %all-to-all-done.8 = bf16[4,2,294912]{2,1,0:T(2,128)(2,1)} async-done(((bf16[4,2,294912]{2,1,0:T(2,128)(2,1)}), bf16[4,2,294912]{2,1,0:T(2,128)(2,1)}, u32[]{:S(2)}, u32[]{:S(2)}) %all-to-all-start.8) | async-done | bytes 4718624 | tf_op jit(solution)/shard_map/all_to_all | solution.py:51
  686.7 10.2 %reshape.156 = bf16[384,48,2,64]{3,2,1,0:T(2,128)(2,1)} reshape(bf16[4,2,294912]{2,1,0:T(2,128)(2,1)} %all-to-all-done.8) | data formatting | bytes 9437184
  696.8 21.4 %copy.181 = bf16[48,4,96,2,64]{2,4,1,3,0:T(8,128)(2,1)} copy(bf16[48,4,96,2,64]{4,3,0,2,1:T(2,128)(2,1)} %bitcast.246) | data formatting | bytes 9437184 | tf_op jit(solution)/shard_map/all_to_all | solution.py:51
  730.4 129.3 %all-reduce.3.cloned.1.call-done = (f32[2,256,256]{2,1,0:T(8,128)}, f32[3,256,256]{2,1,0:T(8,128)}) async-done(((f32[2,256,256]{2,1,0:T(8,128)}, f32[3,256,256]{2,1,0:T(8,128)}), (f32[2,256,256]{2,1,0:T(8,128)}, f32[3,256,256]{2,1,0:T(8,128)})) %all-reduce.3.cloned.1.call-update) | async-done | bytes 1310736 | tf_op jit(solution)/shard_map/psum | solution.py:151
  (128 shorter events, 197.4 us)
Async XLA Ops:
  7.2 72.6 %copy-start = (bf16[48,64,384]{2,1,0:T(8,128)(2,1)S(1)}, bf16[48,64,384]{2,1,0:T(8,128)(2,1)}, u32[]{:S(2)}) copy-start(bf16[48,64,384]{2,1,0:T(8,128)(2,1)} %param.11) | copy-start | bytes 7077892
  7.2 8.0 copy-start.14
  10.2 24.3 %all-to-all-start = ((bf16[8,360,256]{1,0,2:T(8,128)(2,1)}), bf16[8,360,256]{1,0,2:T(8,128)(2,1)}, u32[]{:S(2)}, u32[]{:S(2)}) async-start(bf16[8,360,256]{1,0,2:T(8,128)(2,1)} %copy.145), calls=%async_computation | async-start | bytes 3145728 | tf_op jit(solution)/shard_map/all_to_all | solution.py:78
  42.3 3.1 copy-start.15
  54.7 23.2 %all-to-all-start.1 = ((bf16[8,2,24576]{2,1,0:T(2,128)(2,1)}), bf16[8,2,24576]{2,1,0:T(2,128)(2,1)S(1)}, u32[]{:S(2)}, u32[]{:S(2)}) async-start(bf16[8,2,24576]{2,1,0:T(2,128)(2,1)} %reshape.145), calls=%async_computation.1 | async-start | bytes 1572864 | tf_op jit(solution)/shard_map/all_to_all | solution.py:86
  213.4 4.6 copy-start.12
  217.9 4.8 copy-start.1
  287.6 85.2 %all-to-all-start.3 = ((bf16[48,96,2,256]{1,2,0,3:T(2,128)(2,1)}), bf16[48,96,2,256]{1,2,0,3:T(2,128)(2,1)}, u32[]{:S(2)}, u32[]{:S(2)}) async-start(bf16[48,96,2,256]{1,2,0,3:T(2,128)(2,1)} %pad_maximum_fusion), calls=%async_computation.3 | async-start | bytes 12582912 | tf_op jit(solution)/shard_map/all_to_all | solution.py:101
  293.8 78.5 %copy-start.17 = (s32[1,3]{1,0:T(1,128)S(1)}, s32[1,3]{1,0:T(1,128)}, u32[]{:S(2)}) copy-start(s32[1,3]{1,0:T(1,128)} %param.14) | copy-start | bytes 40
  293.8 78.5 %copy-start.16 = (bf16[3,8,3,8]{3,1,2,0:T(8,128)(2,1)S(1)}, bf16[3,8,3,8]{3,1,2,0:T(8,128)(2,1)}, u32[]{:S(2)}) copy-start(bf16[3,8,3,8]{3,1,2,0:T(8,128)(2,1)} %param.15) | copy-start | bytes 3460
  294.6 67.2 %collective-permute-start = (bf16[8,1,256]{2,0,1:T(8,128)(2,1)S(1)}, bf16[8,1,256]{2,0,1:T(8,128)(2,1)S(1)}, u32[]{:S(2)}, u32[]{:S(2)}) collective-permute-start(bf16[8,1,256]{2,0,1:T(8,128)(2,1)S(1)} %copy.218), channel_id=1, source_target_pairs={{0,1},{1,2},{2,3},{3,0},{4,5},{5,6},{6,7},{7,4},{8,9},{9,10},{10,1... | collective-permute-start | bytes 12296 | tf_op jit(solution)/shard_map/ppermute | solution.py:14
  296.3 69.0 %collective-permute-start.1 = (bf16[8,1,256]{2,0,1:T(8,128)(2,1)S(1)}, bf16[8,1,256]{2,0,1:T(8,128)(2,1)S(1)}, u32[]{:S(2)}, u32[]{:S(2)}) collective-permute-start(bf16[8,1,256]{2,0,1:T(8,128)(2,1)S(1)} %copy.219), channel_id=1, source_target_pairs={{1,0},{2,1},{3,2},{0,3},{5,4},{6,5},{7,6},{4,7},{9,8},{10,9},{11,1... | collective-permute-start | bytes 12296 | tf_op jit(solution)/shard_map/ppermute | solution.py:15
  365.9 63.4 %collective-permute-start.2 = (bf16[8,362,256]{2,0,1:T(8,128)(2,1)}, bf16[8,362,256]{2,0,1:T(8,128)(2,1)}, u32[]{:S(2)}, u32[]{:S(2)}) collective-permute-start(bf16[8,362,256]{2,0,1:T(8,128)(2,1)} %constant_dynamic-update-slice_fusion), channel_id=1, source_target_pairs={{0,4},{4,8},{8,12},{12,16},{16,20},{20,24},{24,28},{1,5},{5,9},{9,... | collective-permute-start | bytes 4448264 | tf_op jit(solution)/shard_map/ppermute | solution.py:14
  369.2 69.1 %collective-permute-start.3 = (bf16[8,362,256]{2,0,1:T(8,128)(2,1)}, bf16[8,362,256]{2,0,1:T(8,128)(2,1)}, u32[]{:S(2)}, u32[]{:S(2)}) collective-permute-start(bf16[8,362,256]{2,0,1:T(8,128)(2,1)} %constant_dynamic-update-slice_fusion), channel_id=1, source_target_pairs={{4,0},{8,4},{12,8},{16,12},{20,16},{24,20},{28,24},{5,1},{9,5},{13... | collective-permute-start | bytes 4448264 | tf_op jit(solution)/shard_map/ppermute | solution.py:15
  422.8 26.9 %all-to-all-start.4 = ((bf16[8,2,24576]{2,1,0:T(2,128)(2,1)}), bf16[8,2,24576]{2,1,0:T(2,128)(2,1)S(1)}, u32[]{:S(2)}, u32[]{:S(2)}) async-start(bf16[8,2,24576]{2,1,0:T(2,128)(2,1)} %reshape.149), calls=%async_computation.4 | async-start | bytes 1572864 | tf_op jit(solution)/shard_map/all_to_all | solution.py:106
  441.8 2.6 copy-start.5
  444.4 2.6 copy-start.7
  447.0 1.2 copy-start.9
  458.7 4.4 copy-start.11
  477.0 23.4 %all-to-all-start.5 = ((bf16[4,2,92160]{2,1,0:T(2,128)(2,1)}), bf16[4,2,92160]{2,1,0:T(2,128)(2,1)}, u32[]{:S(2)}, u32[]{:S(2)}) async-start(bf16[4,2,92160]{2,1,0:T(2,128)(2,1)} %reshape.151), calls=%async_computation.5 | async-start | bytes 2949120 | tf_op jit(solution)/shard_map/all_to_all | solution.py:113
  482.2 2.1 copy-start.3
  482.2 2.1 copy-start.13
  484.3 1.4 copy-start.4
  627.3 59.4 %all-to-all-start.8 = ((bf16[4,2,294912]{2,1,0:T(2,128)(2,1)}), bf16[4,2,294912]{2,1,0:T(2,128)(2,1)}, u32[]{:S(2)}, u32[]{:S(2)}) async-start(bf16[4,2,294912]{2,1,0:T(2,128)(2,1)} %reshape.155), calls=%async_computation.8 | async-start | bytes 9437184 | tf_op jit(solution)/shard_map/all_to_all | solution.py:51
  633.6 226.2 %all-reduce.3.cloned.1.call-start = ((), (), s32[]{:S(2)}) async-start(), calls=%async_computation.9 | async-start | bytes 2621440 | tf_op jit(solution)/shard_map/psum | solution.py:151
  633.6 2.7 copy-start.8
  633.6 2.7 copy-start.10
  636.4 1.4 copy-start.6
  718.3 8.1 slice-start
  722.3 4.1 slice-start.1
  722.3 5.2 copy-start.2
Sparse Core Ops, SparseCore 0:
  730.6 129.1 all-reduce.2
where the time goes:
time: 889 us; the launch traced here: 871 us
  local copies, waits for them, and re-layouts  310 us (35%)
  waiting for transfers between devices  289 us (33%)
  blocking collectives  108 us (12%)
  matrix products  64.3 us (7%)
  starting transfers between devices  42.8 us (5%)
  other arithmetic  42.3 us (5%)
  between operations  14.7 us (2%)
    psum x1, waiting for transfers between devices, local(): grad_spectral = lax.psum(jnp.stack([g_real, g_imag]), ('lat', 'lon'))  129 us
    unnamed x61, local copies, waits for them, and re-layouts  89.4 us
    ppermute x2, waiting for transfers between devices, padded(): before = lax.ppermute(last, axis, up)  65.5 us
    all_to_all x1, blocking collectives, to_degrees(): lax.all_to_all(values, 'lon', split_axis=1, concat_axis=3, tiled=True)  60 us
    all_to_all x1, waiting for transfers between devices, to_degrees(): lax.all_to_all(values, 'lon', split_axis=1, concat_axis=3, tiled=True)  47.2 us
    all_to_all x2, local copies, waits for them, and re-layouts, to_degrees(): lax.all_to_all(values, 'lon', split_axis=1, concat_axis=3, tiled=True)  42.8 us
    convert_element_type x2, local copies, waits for them, and re-layouts, legendre_forward(): return (coeffs * degree_mask[:, :, None, None]).astype(bf16)  40.7 us
    all_to_all x3, local copies, waits for them, and re-layouts, local(): lax.all_to_all(mixed_degrees, 'lon', split_axis=3, concat_axis=1, tiled=T...  37 us
  transfers between devices with their start and end apart: 11, of which 7 were waited for; matrix products, arithmetic and copies ran while one was open for 9% of the time, Pallas kernels for 0%

commit v1 on v0

v1 whole, which is shorter than its diff:
```python
import jax
import jax.numpy as jnp
from jax import lax
from jax.sharding import PartitionSpec as P

BOTH = ("lat", "lon")


def padded(value, sides, width, wrap):
    for axis, dim in sides:
        size, length = (lax.axis_size(axis), value.shape[dim])
        up = [(i, (i + 1) % size) for i in range(size if wrap else size - 1)]
        down = [(j, i) for i, j in up]
        last = lax.slice_in_dim(value, length - width, length, axis=dim)
        leading = lax.slice_in_dim(value, 0, width, axis=dim)
        before = lax.ppermute(last, axis, up)
        after = lax.ppermute(leading, axis, down)
        value = jnp.concatenate([before, value, after], axis=dim)
    return value


def outer_sum(left, right):
    return lax.dot_general(
        left, right, (((0,), (0,)), ((), ())), preferred_element_type=jnp.float32
    )


def local(
    field,
    cotangent,
    legendre,
    quad_weight,
    order_slots,
    support_blocks,
    filter_values,
    spectral_weight,
    disco_weight,
):
    f32 = jnp.float32
    bf16 = jnp.bfloat16
    lat_rows, lon_cols, channels = field.shape
    n_lon = lax.axis_size("lon")
    n_dev = n_lon * lax.axis_size("lat")
    nlon = lon_cols * n_lon
    slots_dev, nlat, degrees = legendre.shape
    own_rows = lat_rows // n_lon
    lat_pos = lax.axis_index("lat")
    lon_pos = lax.axis_index("lon")
    own = -(-slots_dev // n_lon)
    pad = own * n_lon - slots_dev

    orders = order_slots.reshape(-1, slots_dev)
    orders = jnp.pad(orders, ((0, 0), (0, pad))).reshape(n_dev, own)
    flat_orders = orders.reshape(-1)
    column = jnp.arange(nlon, dtype=jnp.int32)
    phase = column[:, None] * flat_orders[None, :] % nlon
    angle = phase.astype(f32) * (2.0 * jnp.pi / nlon)
    cosine = jnp.cos(angle).astype(bf16).reshape(nlon, n_dev, own)
    sine = (-jnp.sin(angle)).astype(bf16).reshape(nlon, n_dev, own)
    table = jnp.stack([cosine, sine], axis=2)
    factor = jnp.where(flat_orders == 0, 1.0, 2.0).astype(bf16).reshape(n_dev, own)

    own_leg = jnp.pad(legendre, ((0, pad), (0, 0), (0, 0)))
    own_leg = lax.dynamic_slice_in_dim(own_leg, lon_pos * own, own)
    own_orders = lax.dynamic_slice_in_dim(orders, lat_pos * n_lon + lon_pos, 1)[0]
    mask = jnp.arange(degrees, dtype=jnp.int32)[None, :] >= own_orders[:, None]
    masked = jnp.where(mask[:, None, :], own_leg, jnp.zeros((), bf16))
    gram = jnp.einsum("kal,kbl->kab", own_leg, masked, preferred_element_type=f32).astype(bf16)

    parts = field.reshape(n_lon, own_rows, lon_cols, channels)
    slabs = lax.all_to_all(parts, "lon", split_axis=0, concat_axis=0, tiled=True)
    slabs = slabs.transpose(1, 0, 2, 3).reshape(own_rows, nlon, channels)
    own_quad = lax.dynamic_slice_in_dim(quad_weight, lon_pos * own_rows, own_rows)
    spectrum = jnp.einsum(
        "ajc,jq->aqc", slabs, table.reshape(nlon, -1), preferred_element_type=f32
    )
    spectrum = (spectrum * (own_quad * (1.0 / nlon))[:, None, None]).astype(bf16)
    spectrum = spectrum.reshape(own_rows, n_dev, 2 * own, channels).transpose(1, 0, 2, 3)
    gathered = lax.all_to_all(spectrum, BOTH, split_axis=0, concat_axis=0, tiled=True)
    gathered = gathered.reshape(nlat, 2, own, channels)
    grid = jnp.einsum("kab,brkc->arkc", gram, gathered, preferred_element_type=f32).astype(bf16)
    grid = grid.reshape(n_dev, own_rows, 2 * own, channels)
    grid = lax.all_to_all(grid, BOTH, split_axis=0, concat_axis=0, tiled=True)
    grid = grid.transpose(1, 0, 2, 3).reshape(own_rows, n_dev * 2 * own, channels)
    grid = lax.all_gather(grid, "lon", axis=0, tiled=True)

    here = lax.dynamic_slice_in_dim(table, lon_pos * lon_cols, lon_cols)
    here = here * factor[None, :, None, :]
    turned = jnp.stack([here[:, :, 1], -here[:, :, 0]], axis=2)
    direct = here.reshape(lon_cols, -1)
    turned = turned.reshape(lon_cols, -1)
    waves = [
        jnp.einsum("jq,aqc->ajc", piece, grid, preferred_element_type=f32).astype(bf16)
        for piece in (direct, turned)
    ]

    rimmed = padded(field, (("lon", 1),), 1, True)
    extended = padded(rimmed, (("lat", 0),), lat_rows, False)
    picks = support_blocks[0] - lat_pos + 1
    onehot = (picks[:, None] == jnp.arange(3, dtype=jnp.int32)[None, :]).astype(f32)
    operator = (
        jnp.einsum("tasb,sq->taqb", filter_values.astype(f32), onehot)
        .reshape(3, lat_rows, 3 * lat_rows)
        .astype(bf16)
    )
    responses = []
    for tap in range(3):
        window = extended[:, tap : tap + lon_cols]
        responses.append(
            jnp.einsum("ab,boc->aoc", operator[tap], window, preferred_element_type=f32).astype(
                bf16
            )
        )
    sources = [v.reshape(-1, channels) for v in waves + responses]
    weights = [spectral_weight[0], spectral_weight[1]] + [disco_weight[t] for t in range(3)]
    pre_act = sum(
        jnp.dot(s, w, preferred_element_type=f32) for s, w in zip(sources, weights)
    ).reshape(lat_rows, lon_cols, channels)
    activated, pullback = jax.vjp(jax.nn.gelu, pre_act)
    output = (field.astype(f32) + activated).astype(bf16)
    (grad_pre,) = pullback(cotangent.astype(f32))
    flat_grad = grad_pre.astype(bf16).reshape(-1, channels)
    grads = jnp.concatenate([outer_sum(s, flat_grad) for s in sources], axis=0)
    grads = grads.astype(bf16).reshape(n_dev, -1, channels)
    terms = lax.all_to_all(grads, BOTH, split_axis=0, concat_axis=0, tiled=True)
    total = jnp.sum(terms.astype(f32), axis=0).astype(bf16)
    total = lax.all_gather(total, BOTH, axis=0, tiled=True).astype(f32)
    total = total.reshape(5, channels, channels)
    return (output, total[:2], total[2:])


def solution(mesh):
    placed = (
        P("lat", "lon", None),
        P("lat", "lon", None),
        P("lat", None, None),
        P("lat"),
        P(),
        P("lat", None),
        P(None, "lat", None, None),
        P(),
        P(),
    )
    return jax.shard_map(
        local,
        mesh=mesh,
        in_specs=placed,
        out_specs=(P("lat", "lon", None), P(), P()),
        check_vma=False,
    )
```

time: 889 us -> 283 us (0.32)
  the two profiles are of different devices: /device:TPU:25 before, /device:TPU:0 now
where the time goes in v1:
time: 283 us; the launch traced here: 282 us
  blocking collectives  86.7 us (31%)
  waiting for transfers between devices  75.6 us (27%)
  local copies, waits for them, and re-layouts  42.1 us (15%)
  other arithmetic  24.8 us (9%)
  starting transfers between devices  20.2 us (7%)
  matrix products  18.3 us (6%)
  between operations  14.4 us (5%)
    ppermute x2, waiting for transfers between devices, padded(): before = lax.ppermute(last, axis, up)  55.1 us
    all_gather x1, blocking collectives, local(): total = lax.all_gather(total, BOTH, axis=0, tiled=True).astype(f32)  41.2 us
    all_to_all x1, blocking collectives, local(): grid = lax.all_to_all(grid, BOTH, split_axis=0, concat_axis=0, tiled=True)  24 us
    all_to_all x1, blocking collectives, local(): terms = lax.all_to_all(grads, BOTH, split_axis=0, concat_axis=0, tiled=True)  21.4 us
    all_to_all x1, waiting for transfers between devices, local(): lax.all_to_all(spectrum, BOTH, split_axis=0, concat_axis=0, tiled=True)  20.5 us
    convert_element_type x1, other arithmetic, local(): cosine = jnp.cos(angle).astype(bf16).reshape(nlon, n_dev, own)  13.9 us
    unnamed x42, local copies, waits for them, and re-layouts  11.3 us
    all_to_all x1, starting transfers between devices, local(): lax.all_to_all(spectrum, BOTH, split_axis=0, concat_axis=0, tiled=True)  7.88 us
  transfers between devices with their start and end apart: 7, of which 3 were waited for; matrix products, arithmetic and copies ran while one was open for 14% of the time, Pallas kernels for 0%

profile of v1, /device:TPU:0, one launch (start us, length us, event | category | flops | bytes accessed | tf_op | source)
XLA Modules:
  0.0 282.1 jit_solution(17866680132580840743)
XLA Ops:
  7.2 4.5 %all-to-all-start = ((bf16[4,2,360,256]{3,2,1,0:T(8,128)(2,1)}), bf16[4,2,360,256]{3,2,1,0:T(8,128)(2,1)}, u32[]{:S(2)}, u32[]{:S(2)}) async-start(bf16[4,2,360,256]{3,2,1,0:T(8,128)(2,1)} %bitcast.144), calls=%async_computation | async-start | bytes 2949120 | tf_op jit(solution)/shard_map/all_to_all | solution.py:71
  11.8 13.9 %cosine_convert_fusion = (bf16[1440,32,1,12]{0,3,2,1:T(8,128)(2,1)S(1)}, bf16[1440,32,1,12]{0,3,2,1:T(8,128)(2,1)S(1)}) fusion(s32[32,12]{1,0:T(8,128)S(1)} %mul.122), kind=kLoop, calls=%fused_computation.22 | loop fusion | flops 6635520 | bytes 2213376 | tf_op jit(solution)/shard_map/convert_element_type | solution.py:58
  25.7 2.1 pad_maximum_fusion.1
  27.8 5.2 %reshape.167 = bf16[1440,768]{0,1:T(8,128)(2,1)} reshape(bf16[1440,32,2,12]{0,3,2,1:T(8,128)(2,1)} %pad_maximum_fusion.1) | data formatting | bytes 4423680 | tf_op jit(solution)/shard_map/reshape | solution.py:75
  33.1 1.6 copy.38
  35.2 1.4 multiply_convert_fusion
  36.6 1.7 copy.80
  38.3 7.9 %all-to-all-start.1 = ((bf16[32,2,24,256]{3,1,2,0:T(2,128)(2,1)}), bf16[32,2,24,256]{3,1,2,0:T(2,128)(2,1)}, u32[]{:S(2)}, u32[]{:S(2)}) async-start(bf16[32,2,24,256]{3,1,2,0:T(2,128)(2,1)} %bitcast.149), calls=%async_computation.1 | async-start | bytes 1572864 | tf_op jit(solution)/shard_map/all_to_all | solution.py:79
  46.3 20.5 %all-to-all-done.1 = bf16[32,2,24,256]{3,1,2,0:T(2,128)(2,1)} async-done(((bf16[32,2,24,256]{3,1,2,0:T(2,128)(2,1)}), bf16[32,2,24,256]{3,1,2,0:T(2,128)(2,1)}, u32[]{:S(2)}, u32[]{:S(2)}) %all-to-all-start.1) | async-done | bytes 786464 | tf_op jit(solution)/shard_map/all_to_all | solution.py:79
  66.8 2.8 %copy.41 = bf16[32,2,24,256]{3,1,0,2:T(2,128)(2,1)} copy(bf16[32,2,24,256]{3,1,2,0:T(2,128)(2,1)} %all-to-all-done.1) | data formatting | bytes 1572864 | tf_op jit(solution)/shard_map/all_to_all | solution.py:79
  69.6 3.0 %reshape.171 = bf16[64,2,12,256]{3,0,2,1:T(8,128)(2,1)} reshape(bf16[32,2,24,256]{3,1,0,2:T(2,128)(2,1)} %copy.41) | data formatting | bytes 1572864 | tf_op jit(solution)/shard_map/reshape | solution.py:80
  72.6 2.9 %fusion.38 = bf16[64,2,12,256]{3,0,1,2:T(8,128)(2,1)} fusion(bf16[64,2,12,256]{3,0,2,1:T(8,128)(2,1)} %reshape.171, bf16[48,64,384]{2,1,0:T(8,128)(2,1)} %param.11, s32[]{:T(128)S(6)} %select_n.40, pred[12,384]{1,0:T(8,128)(4,1)S(1)} %iota_compare_fusion), kind=kOutput, calls=%fused_computation.51 | convolution fusion | flops 88817664 | bytes 2758144 | tf_op jit(solution)/shard_map/kab,brkc->arkc/dot_general | solution.py:81
  75.5 2.1 copy.43
  77.6 2.8 %reshape.172 = bf16[32,2,24,256]{3,1,0,2:T(2,128)(2,1)} reshape(bf16[64,2,12,256]{3,0,2,1:T(8,128)(2,1)} %copy.43) | data formatting | bytes 1572864 | tf_op jit(solution)/shard_map/reshape | solution.py:82
  80.4 1.7 copy.44
  82.1 24.0 %all_to_all.20 = bf16[32,2,24,256]{3,1,2,0:T(2,128)(2,1)S(1)} all-to-all(bf16[32,2,24,256]{3,1,2,0:T(2,128)(2,1)S(1)} %copy.44), channel_id=1, replica_groups=mesh['lat'=8,'lon'=4] {'lat','lon'}, dimensions={0} | all-to-all | bytes 1572864 | tf_op jit(solution)/shard_map/all_to_all | solution.py:83
  108.0 1.7 collective-permute-start.1
  109.8 1.3 collective-permute-done
  111.6 2.9 %constant_dynamic-update-slice_fusion.1 = bf16[8,362,256]{2,0,1:T(8,128)(2,1)} fusion(bf16[8,362,256]{2,0,1:T(8,128)(2,1)} %constant_dynamic-update-slice_fusion.2, bf16[8,360,256]{2,1,0:T(8,128)(2,1)} %param.9), kind=kLoop, calls=%fused_computation.100 | loop fusion | bytes 2949120
  115.1 4.6 %collective-permute-start.2 = (bf16[8,362,256]{2,0,1:T(8,128)(2,1)}, bf16[8,362,256]{2,0,1:T(8,128)(2,1)}, u32[]{:S(2)}, u32[]{:S(2)}) collective-permute-start(bf16[8,362,256]{2,0,1:T(8,128)(2,1)} %constant_dynamic-update-slice_fusion), channel_id=1, source_target_pairs={{0,4},{4,8},{8,12},{12,16},{16,20},{20,24},{24,28},{1,5},{5,9},{9,... | collective-permute-start | bytes 4448264 | tf_op jit(solution)/shard_map/ppermute | solution.py:16
  119.8 1.5 collective-permute-start.3
  121.3 1.4 fusion.72
  122.8 2.1 reshape.174
  124.9 1.2 fusion.103
  127.9 53.8 %collective-permute-done.2 = bf16[8,362,256]{2,0,1:T(8,128)(2,1)} collective-permute-done((bf16[8,362,256]{2,0,1:T(8,128)(2,1)}, bf16[8,362,256]{2,0,1:T(8,128)(2,1)}, u32[]{:S(2)}, u32[]{:S(2)}) %collective-permute-start.2) | collective-permute-done | bytes 1482784 | tf_op jit(solution)/shard_map/ppermute | solution.py:16
  181.7 2.4 pad_maximum_fusion
  188.9 1.4 copy.54
  190.3 3.4 %convolution_convert_fusion.1 = bf16[8,256,360]{1,2,0:T(8,128)(2,1)S(1)} fusion(bf16[8,768,256]{2,1,0:T(8,128)(2,1)} %all-gather.2.cloned.1.call-done, bf16[360,768]{0,1:T(8,128)(2,1)} %reshape.174), kind=kOutput, calls=%fused_computation.41 | convolution fusion | flops 1133199360 | bytes 5173248 | tf_op jit(solution)/shard_map/jq,aqc->ajc/dot_general | solution.py:93
  195.8 1.4 convolution_convert_fusion
  201.9 3.3 %fusion.13 = (bf16[8,360,256]{2,1,0:T(8,128)(2,1)S(1)}, bf16[8,360,256]{2,1,0:T(8,128)(2,1)}) fusion(bf16[8,360,256]{2,1,0:T(8,128)(2,1)S(1)} %copy-done.11, f32[8,360,256]{2,1,0:T(8,128)S(1)} %bitcast.145, bf16[8,360,256]{2,1,0:T(8,128)(2,1)S(1)} %copy-done.2), kind=kLoop, calls=%fused_computation.29 | loop fusion | flops 18432000 | bytes 8847360 | tf_op jit(solution)/shard_map/convert_element_type | solution.py:122
  210.8 21.4 %all_to_all.21 = bf16[32,40,256]{2,1,0:T(8,128)(2,1)S(1)} all-to-all(bf16[32,40,256]{2,1,0:T(8,128)(2,1)S(1)} %bitcast.156), channel_id=1, replica_groups=mesh['lat'=8,'lon'=4] {'lat','lon'}, dimensions={0} | all-to-all | bytes 1310720 | tf_op jit(solution)/shard_map/all_to_all | solution.py:125
  232.3 41.2 %all_gather.7 = bf16[1280,256]{1,0:T(8,128)(2,1)S(1)} all-gather(bf16[40,256]{1,0:T(8,128)(2,1)S(1)} %reduce_sum.12), channel_id=1, replica_groups=mesh['lat'=8,'lon'=4] {'lat','lon'}, dimensions={0}, use_global_device_ids=true | all-gather | bytes 675840 | tf_op jit(solution)/shard_map/all_gather | solution.py:127
  (83 shorter events, 24.5 us)
Async XLA Ops:
  7.2 120.3 %copy-start = (bf16[3,8,3,8]{3,1,2,0:T(8,128)(2,1)S(1)}, bf16[3,8,3,8]{3,1,2,0:T(8,128)(2,1)}, u32[]{:S(2)}) copy-start(bf16[3,8,3,8]{3,1,2,0:T(8,128)(2,1)} %param.15) | copy-start | bytes 3460
  7.2 4.5 %copy-start.15 = (s32[384]{0:T(512)S(1)}, s32[384]{0:T(512)}, u32[]{:S(2)}) copy-start(s32[384]{0:T(512)} %param.13) | copy-start | bytes 4612
  7.2 25.9 %all-to-all-start = ((bf16[4,2,360,256]{3,2,1,0:T(8,128)(2,1)}), bf16[4,2,360,256]{3,2,1,0:T(8,128)(2,1)}, u32[]{:S(2)}, u32[]{:S(2)}) async-start(bf16[4,2,360,256]{3,2,1,0:T(8,128)(2,1)} %bitcast.144), calls=%async_computation | async-start | bytes 2949120 | tf_op jit(solution)/shard_map/all_to_all | solution.py:71
  27.8 5.2 %copy-start.17 = (f32[8]{0:T(128)S(1)}, f32[8]{0:T(128)}, u32[]{:S(2)}) copy-start(f32[8]{0:T(128)} %param.12) | copy-start | bytes 100
  33.1 2.1 copy-start.10
  38.3 28.5 %all-to-all-start.1 = ((bf16[32,2,24,256]{3,1,2,0:T(2,128)(2,1)}), bf16[32,2,24,256]{3,1,2,0:T(2,128)(2,1)}, u32[]{:S(2)}, u32[]{:S(2)}) async-start(bf16[32,2,24,256]{3,1,2,0:T(2,128)(2,1)} %bitcast.149), calls=%async_computation.1 | async-start | bytes 1572864 | tf_op jit(solution)/shard_map/all_to_all | solution.py:79
  46.2 144.1 %all-gather.2.cloned.1.call-start = ((), (), s32[]{:S(2)}) async-start(), calls=%async_computation.4 | async-start | bytes 3932160 | tf_op jit(solution)/shard_map/all_gather | solution.py:85
  108.0 3.1 %collective-permute-start = (bf16[8,1,256]{2,0,1:T(8,128)(2,1)S(1)}, bf16[8,1,256]{2,0,1:T(8,128)(2,1)S(1)}, u32[]{:S(2)}, u32[]{:S(2)}) collective-permute-start(bf16[8,1,256]{2,0,1:T(8,128)(2,1)S(1)} %copy.78), channel_id=1, source_target_pairs={{0,1},{1,2},{2,3},{3,0},{4,5},{5,6},{6,7},{7,4},{8,9},{9,10},{10,1... | collective-permute-start | bytes 12296 | tf_op jit(solution)/shard_map/ppermute | solution.py:16
  108.0 6.5 %collective-permute-start.1 = (bf16[8,1,256]{2,0,1:T(8,128)(2,1)S(1)}, bf16[8,1,256]{2,0,1:T(8,128)(2,1)S(1)}, u32[]{:S(2)}, u32[]{:S(2)}) collective-permute-start(bf16[8,1,256]{2,0,1:T(8,128)(2,1)S(1)} %copy.79), channel_id=1, source_target_pairs={{1,0},{2,1},{3,2},{0,3},{5,4},{6,5},{7,6},{4,7},{9,8},{10,9},{11,1... | collective-permute-start | bytes 12296 | tf_op jit(solution)/shard_map/ppermute | solution.py:17
  115.1 66.5 %collective-permute-start.2 = (bf16[8,362,256]{2,0,1:T(8,128)(2,1)}, bf16[8,362,256]{2,0,1:T(8,128)(2,1)}, u32[]{:S(2)}, u32[]{:S(2)}) collective-permute-start(bf16[8,362,256]{2,0,1:T(8,128)(2,1)} %constant_dynamic-update-slice_fusion), channel_id=1, source_target_pairs={{0,4},{4,8},{8,12},{12,16},{16,20},{20,24},{24,28},{1,5},{5,9},{9,... | collective-permute-start | bytes 4448264 | tf_op jit(solution)/shard_map/ppermute | solution.py:16
  119.8 61.9 %collective-permute-start.3 = (bf16[8,362,256]{2,0,1:T(8,128)(2,1)}, bf16[8,362,256]{2,0,1:T(8,128)(2,1)}, u32[]{:S(2)}, u32[]{:S(2)}) collective-permute-start(bf16[8,362,256]{2,0,1:T(8,128)(2,1)} %constant_dynamic-update-slice_fusion), channel_id=1, source_target_pairs={{4,0},{8,4},{12,8},{16,12},{20,16},{24,20},{28,24},{5,1},{9,5},{13... | collective-permute-start | bytes 4448264 | tf_op jit(solution)/shard_map/ppermute | solution.py:17
  124.9 2.5 copy-start.18
  185.1 1.3 copy-start.4
  186.4 1.3 copy-start.6
  187.7 1.2 copy-start.8
  190.3 3.4 %copy-start.14 = (bf16[2,256,256]{2,1,0:T(8,128)(2,1)S(1)}, bf16[2,256,256]{2,1,0:T(8,128)(2,1)}, u32[]{:S(2)}) copy-start(bf16[2,256,256]{2,1,0:T(8,128)(2,1)} %param.16) | copy-start | bytes 786436
  193.7 1.1 copy-start.12
  193.7 2.1 copy-start.16
  197.1 1.0 copy-start.13
  198.7 1.4 copy-start.3
  200.1 1.4 copy-start.2
  200.1 1.8 copy-start.11
  205.9 1.4 copy-start.5
  207.3 1.4 copy-start.7
  208.6 1.4 copy-start.9
  210.8 64.5 %copy-start.1 = (bf16[3,8,3,8]{3,1,2,0:T(8,128)(2,1)S(1)}, bf16[3,8,3,8]{3,1,2,0:T(8,128)(2,1)}, u32[]{:S(2)}) copy-start(bf16[3,8,3,8]{3,1,2,0:T(8,128)(2,1)} %param.15) | copy-start | bytes 3460
Sparse Core Ops, SparseCore 0:
  107.3 27.5 all-gather.1

commit v2 on v1

--- a/solution.py
+++ b/solution.py
@@ -1,7 +1,13 @@
+import functools
+
 import jax
 import jax.numpy as jnp
 from jax import lax
+from jax.experimental import pallas as pl
+from jax.experimental.pallas import tpu as pltpu
 from jax.sharding import PartitionSpec as P
+
+MESH = pl.DeviceIdType.MESH
 
 BOTH = ("lat", "lon")
 
@@ -17,6 +23,101 @@
         after = lax.ppermute(leading, axis, down)
         value = jnp.concatenate([before, value, after], axis=dim)
     return value
+
+
+def greet_all(n, n_lon, me):
+    barrier = pltpu.get_barrier_semaphore()
+
+    def signal(step, carry):
+        d = lax.rem(me + step, n)
+        pl.semaphore_signal(
+            barrier, inc=1, device_id=(d // n_lon, lax.rem(d, n_lon)), device_id_type=MESH
+        )
+        return carry
+
+    lax.fori_loop(1, n, signal, 0)
+    pl.semaphore_wait(barrier, n - 1)
+
+
+def push(src, dst, send_sem, recv_sem, d, n_lon):
+    return pltpu.make_async_remote_copy(
+        src_ref=src,
+        dst_ref=dst,
+        send_sem=send_sem,
+        recv_sem=recv_sem,
+        device_id=(d // n_lon, lax.rem(d, n_lon)),
+        device_id_type=MESH,
+    )
+
+
+def reduce_kernel(n, n_lon, x_ref, out_ref, parts, total, gath, s1, r1, s2, r2):
+    me = lax.axis_index("lat") * n_lon + lax.axis_index("lon")
+    greet_all(n, n_lon, me)
+
+    def scatter(step, carry):
+        d = lax.rem(me + step, n)
+        push(x_ref.at[d], parts.at[me], s1.at[d], r1.at[me], d, n_lon).start()
+        return carry
+
+    lax.fori_loop(1, n, scatter, 0)
+
+    def add(step, acc):
+        d = lax.rem(me + n - step, n)
+        push(x_ref.at[d], parts.at[d], s1.at[d], r1.at[d], d, n_lon).wait_recv()
+        return acc + parts[d].astype(jnp.float32)
+
+    total[...] = lax.fori_loop(1, n, add, x_ref[me].astype(jnp.float32)).astype(total.dtype)
+
+    def spread(step, carry):
+        d = lax.rem(me + step, n)
+        push(total, gath.at[me], s2.at[d], r2.at[me], d, n_lon).start()
+        return carry
+
+    lax.fori_loop(1, n, spread, 0)
+    out_ref[me] = total[...].astype(out_ref.dtype)
+
+    def collect(step, carry):
+        d = lax.rem(me + n - step, n)
+        push(total, gath.at[d], s2.at[d], r2.at[d], d, n_lon).wait_recv()
+        out_ref[d] = gath[d].astype(out_ref.dtype)
+        return carry
+
+    lax.fori_loop(1, n, collect, 0)
+
+    def drain(step, carry):
+        d = lax.rem(me + step, n)
+        push(x_ref.at[d], parts.at[me], s1.at[d], r1.at[me], d, n_lon).wait_send()
+        push(total, gath.at[me], s2.at[d], r2.at[me], d, n_lon).wait_send()
+        return carry
+
+    lax.fori_loop(1, n, drain, 0)
+
+
+def reduce_all(values, n, n_lon):
+    size = values.size
+    rows = -(-size // (128 * n * 16)) * 16
+    flat = jnp.pad(values.reshape(-1), (0, rows * 128 * n - size)).reshape(n, rows, 128)
+    vmem = pl.BlockSpec(memory_space=pltpu.VMEM)
+    dma = pltpu.SemaphoreType.DMA((n,))
+    out = pl.pallas_call(
+        functools.partial(reduce_kernel, n, n_lon),
+        out_shape=jax.ShapeDtypeStruct((n, rows, 128), jnp.float32),
+        in_specs=[vmem],
+        out_specs=vmem,
+        scratch_shapes=[
+            pltpu.VMEM((n, rows, 128), jnp.bfloat16),
+            pltpu.VMEM((rows, 128), jnp.bfloat16),
+            pltpu.VMEM((n, rows, 128), jnp.bfloat16),
+            dma,
+            dma,
+            dma,
+            dma,
+        ],
+        compiler_params=pltpu.CompilerParams(
+            collective_id=0, has_side_effects=True, vmem_limit_bytes=32 * 2**20
+        ),
+    )(flat.astype(jnp.bfloat16))
+    return out.reshape(-1)[:size].reshape(values.shape)
 
 
 def outer_sum(left, right):
@@ -121,11 +222,7 @@
     (grad_pre,) = pullback(cotangent.astype(f32))
     flat_grad = grad_pre.astype(bf16).reshape(-1, channels)
     grads = jnp.concatenate([outer_sum(s, flat_grad) for s in sources], axis=0)
-    grads = grads.astype(bf16).reshape(n_dev, -1, channels)
-    terms = lax.all_to_all(grads, BOTH, split_axis=0, concat_axis=0, tiled=True)
-    total = jnp.sum(terms.astype(f32), axis=0).astype(bf16)
-    total = lax.all_gather(total, BOTH, axis=0, tiled=True).astype(f32)
-    total = total.reshape(5, channels, channels)
+    total = reduce_all(grads.reshape(5, channels, channels), n_dev, n_lon)
     return (output, total[:2], total[2:])
 
 

time: 283 us -> 256 us (0.905)
  the two profiles are of different devices: /device:TPU:0 before, /device:TPU:25 now
where the time goes in v2:
time: 256 us; the launch traced here: 255 us
  waiting for transfers between devices  75 us (29%)
  local copies, waits for them, and re-layouts  42.5 us (17%)
  Pallas kernels  36 us (14%)
  other arithmetic  24.7 us (10%)
  blocking collectives  24 us (9%)
  starting transfers between devices  19.5 us (8%)
  matrix products  18.4 us (7%)
  between operations  14.4 us (6%)
    pallas_call x1, Pallas kernels, reduce_all(): pl.pallas_call(functools.partial(reduce_kernel, n, n_lon), out_shape=jax....  36 us
    ppermute x2, waiting for transfers between devices, padded(): after = lax.ppermute(leading, axis, down)  33.2 us
    all_to_all x1, blocking collectives, local(): grid = lax.all_to_all(grid, BOTH, split_axis=0, concat_axis=0, tiled=True)  24 us
    ppermute x2, waiting for transfers between devices, padded(): before = lax.ppermute(last, axis, up)  23.8 us
    all_to_all x1, waiting for transfers between devices, local(): lax.all_to_all(spectrum, BOTH, split_axis=0, concat_axis=0, tiled=True)  18 us
    convert_element_type x1, other arithmetic, local(): cosine = jnp.cos(angle).astype(bf16).reshape(nlon, n_dev, own)  13.9 us
    unnamed x42, local copies, waits for them, and re-layouts  11.1 us
    all_to_all x1, starting transfers between devices, local(): lax.all_to_all(spectrum, BOTH, split_axis=0, concat_axis=0, tiled=True)  6.09 us
  transfers between devices with their start and end apart: 7, of which 4 were waited for; matrix products, arithmetic and copies ran while one was open for 16% of the time, Pallas kernels for 0%

profile of v2, /device:TPU:25, one launch (start us, length us, event | category | flops | bytes accessed | tf_op | source)
XLA Modules:
  0.0 254.5 jit_solution(14794260385886131663)
XLA Ops:
  7.2 5.1 %all-to-all-start = ((bf16[4,2,360,256]{3,2,1,0:T(8,128)(2,1)}), bf16[4,2,360,256]{3,2,1,0:T(8,128)(2,1)}, u32[]{:S(2)}, u32[]{:S(2)}) async-start(bf16[4,2,360,256]{3,2,1,0:T(8,128)(2,1)} %bitcast.141), calls=%async_computation | async-start | bytes 2949120 | tf_op jit(solution)/shard_map/all_to_all | solution.py:172
  12.4 13.9 %cosine_convert_fusion = (bf16[1440,32,1,12]{0,3,2,1:T(8,128)(2,1)S(1)}, bf16[1440,32,1,12]{0,3,2,1:T(8,128)(2,1)S(1)}) fusion(s32[32,12]{1,0:T(8,128)S(1)} %mul.122), kind=kLoop, calls=%fused_computation.22 | loop fusion | flops 6635520 | bytes 2213376 | tf_op jit(solution)/shard_map/convert_element_type | solution.py:159
  26.3 2.1 pad_maximum_fusion.1
  28.4 5.2 %reshape.164 = bf16[1440,768]{0,1:T(8,128)(2,1)} reshape(bf16[1440,32,2,12]{0,3,2,1:T(8,128)(2,1)} %pad_maximum_fusion.1) | data formatting | bytes 4423680 | tf_op jit(solution)/shard_map/reshape | solution.py:176
  33.7 1.6 copy.38
  35.8 1.4 multiply_convert_fusion
  37.2 1.7 copy.80
  38.9 6.1 %all-to-all-start.1 = ((bf16[32,2,24,256]{3,1,2,0:T(2,128)(2,1)}), bf16[32,2,24,256]{3,1,2,0:T(2,128)(2,1)}, u32[]{:S(2)}, u32[]{:S(2)}) async-start(bf16[32,2,24,256]{3,1,2,0:T(2,128)(2,1)} %bitcast.146), calls=%async_computation.1 | async-start | bytes 1572864 | tf_op jit(solution)/shard_map/all_to_all | solution.py:180
  45.2 18.0 %all-to-all-done.1 = bf16[32,2,24,256]{3,1,2,0:T(2,128)(2,1)} async-done(((bf16[32,2,24,256]{3,1,2,0:T(2,128)(2,1)}), bf16[32,2,24,256]{3,1,2,0:T(2,128)(2,1)}, u32[]{:S(2)}, u32[]{:S(2)}) %all-to-all-start.1) | async-done | bytes 786464 | tf_op jit(solution)/shard_map/all_to_all | solution.py:180
  63.1 2.8 %copy.41 = bf16[32,2,24,256]{3,1,0,2:T(2,128)(2,1)} copy(bf16[32,2,24,256]{3,1,2,0:T(2,128)(2,1)} %all-to-all-done.1) | data formatting | bytes 1572864 | tf_op jit(solution)/shard_map/all_to_all | solution.py:180
  66.0 3.0 %reshape.168 = bf16[64,2,12,256]{3,0,2,1:T(8,128)(2,1)} reshape(bf16[32,2,24,256]{3,1,0,2:T(2,128)(2,1)} %copy.41) | data formatting | bytes 1572864 | tf_op jit(solution)/shard_map/reshape | solution.py:181
  68.9 2.9 %fusion.38 = bf16[64,2,12,256]{3,0,1,2:T(8,128)(2,1)} fusion(bf16[64,2,12,256]{3,0,2,1:T(8,128)(2,1)} %reshape.168, bf16[48,64,384]{2,1,0:T(8,128)(2,1)} %param.11, s32[]{:T(128)S(6)} %select_n.40, pred[12,384]{1,0:T(8,128)(4,1)S(1)} %iota_compare_fusion), kind=kOutput, calls=%fused_computation.51 | convolution fusion | flops 88817664 | bytes 2758144 | tf_op jit(solution)/shard_map/kab,brkc->arkc/dot_general | solution.py:182
  71.8 2.1 copy.43
  73.9 2.8 %reshape.169 = bf16[32,2,24,256]{3,1,0,2:T(2,128)(2,1)} reshape(bf16[64,2,12,256]{3,0,2,1:T(8,128)(2,1)} %copy.43) | data formatting | bytes 1572864 | tf_op jit(solution)/shard_map/reshape | solution.py:183
  76.8 1.7 copy.44
  78.5 24.0 %all_to_all.15 = bf16[32,2,24,256]{3,1,2,0:T(2,128)(2,1)S(1)} all-to-all(bf16[32,2,24,256]{3,1,2,0:T(2,128)(2,1)S(1)} %copy.44), channel_id=1, replica_groups=mesh['lat'=8,'lon'=4] {'lat','lon'}, dimensions={0} | all-to-all | bytes 1572864 | tf_op jit(solution)/shard_map/all_to_all | solution.py:184
  104.3 1.9 collective-permute-start
  107.5 2.8 %constant_dynamic-update-slice_fusion.1 = bf16[8,362,256]{2,0,1:T(8,128)(2,1)} fusion(bf16[8,362,256]{2,0,1:T(8,128)(2,1)} %constant_dynamic-update-slice_fusion.2, bf16[8,360,256]{2,1,0:T(8,128)(2,1)} %param.9), kind=kLoop, calls=%fused_computation.100 | loop fusion | bytes 2949120
  110.9 3.1 %collective-permute-start.2 = (bf16[8,362,256]{2,0,1:T(8,128)(2,1)}, bf16[8,362,256]{2,0,1:T(8,128)(2,1)}, u32[]{:S(2)}, u32[]{:S(2)}) collective-permute-start(bf16[8,362,256]{2,0,1:T(8,128)(2,1)} %constant_dynamic-update-slice_fusion), channel_id=1, source_target_pairs={{0,4},{4,8},{8,12},{12,16},{16,20},{20,24},{24,28},{1,5},{5,9},{9,... | collective-permute-start | bytes 4448264 | tf_op jit(solution)/shard_map/ppermute | solution.py:22
  114.0 3.3 %collective-permute-start.3 = (bf16[8,362,256]{2,0,1:T(8,128)(2,1)}, bf16[8,362,256]{2,0,1:T(8,128)(2,1)}, u32[]{:S(2)}, u32[]{:S(2)}) collective-permute-start(bf16[8,362,256]{2,0,1:T(8,128)(2,1)} %constant_dynamic-update-slice_fusion), channel_id=1, source_target_pairs={{4,0},{8,4},{12,8},{16,12},{20,16},{24,20},{28,24},{5,1},{9,5},{13... | collective-permute-start | bytes 4448264 | tf_op jit(solution)/shard_map/ppermute | solution.py:23
  117.4 1.5 fusion.72
  118.9 2.1 reshape.171
  121.0 1.2 fusion.103
  124.0 23.1 %collective-permute-done.2 = bf16[8,362,256]{2,0,1:T(8,128)(2,1)} collective-permute-done((bf16[8,362,256]{2,0,1:T(8,128)(2,1)}, bf16[8,362,256]{2,0,1:T(8,128)(2,1)}, u32[]{:S(2)}, u32[]{:S(2)}) %collective-permute-start.2) | collective-permute-done | bytes 1482784 | tf_op jit(solution)/shard_map/ppermute | solution.py:22
  147.0 33.2 %collective-permute-done.3 = bf16[8,362,256]{2,0,1:T(8,128)(2,1)} collective-permute-done((bf16[8,362,256]{2,0,1:T(8,128)(2,1)}, bf16[8,362,256]{2,0,1:T(8,128)(2,1)}, u32[]{:S(2)}, u32[]{:S(2)}) %collective-permute-start.3) | collective-permute-done | bytes 1482784 | tf_op jit(solution)/shard_map/ppermute | solution.py:23
  180.2 2.4 pad_maximum_fusion
  186.2 1.2 copy-done.8
  187.4 1.4 copy.54
  188.8 3.4 %convolution_convert_fusion.1 = bf16[8,256,360]{1,2,0:T(8,128)(2,1)S(1)} fusion(bf16[8,768,256]{2,1,0:T(8,128)(2,1)} %all-gather.2.cloned.1.call-done, bf16[360,768]{0,1:T(8,128)(2,1)} %reshape.171), kind=kOutput, calls=%fused_computation.41 | convolution fusion | flops 1133199360 | bytes 5173248 | tf_op jit(solution)/shard_map/jq,aqc->ajc/dot_general | solution.py:194
  194.3 1.4 convolution_convert_fusion
  200.4 3.3 %fusion.13 = (bf16[8,360,256]{2,1,0:T(8,128)(2,1)S(1)}, bf16[8,360,256]{2,1,0:T(8,128)(2,1)}) fusion(bf16[8,360,256]{2,1,0:T(8,128)(2,1)S(1)} %copy-done.11, f32[8,360,256]{2,1,0:T(8,128)S(1)} %bitcast.142, bf16[8,360,256]{2,1,0:T(8,128)(2,1)S(1)} %copy-done.2), kind=kLoop, calls=%fused_computation.29 | loop fusion | flops 18432000 | bytes 8847360 | tf_op jit(solution)/shard_map/convert_element_type | solution.py:223
  209.5 36.0 %shard_map.112 = f32[32,80,128]{2,1,0:T(8,128)S(1)} custom-call(bf16[32,80,128]{2,1,0:T(8,128)(2,1)S(1)} %convert_element_type.119.x_ref), custom_call_target="tpu_custom_call" | custom-call | tf_op jit(solution)/shard_map/pallas_call | solution.py:102
  (83 shorter events, 24.5 us)
Async XLA Ops:
  7.2 116.4 %copy-start = (bf16[3,8,3,8]{3,1,2,0:T(8,128)(2,1)S(1)}, bf16[3,8,3,8]{3,1,2,0:T(8,128)(2,1)}, u32[]{:S(2)}) copy-start(bf16[3,8,3,8]{3,1,2,0:T(8,128)(2,1)} %param.15) | copy-start | bytes 3460
  7.2 5.1 %copy-start.15 = (s32[384]{0:T(512)S(1)}, s32[384]{0:T(512)}, u32[]{:S(2)}) copy-start(s32[384]{0:T(512)} %param.13) | copy-start | bytes 4612
  7.2 26.5 %all-to-all-start = ((bf16[4,2,360,256]{3,2,1,0:T(8,128)(2,1)}), bf16[4,2,360,256]{3,2,1,0:T(8,128)(2,1)}, u32[]{:S(2)}, u32[]{:S(2)}) async-start(bf16[4,2,360,256]{3,2,1,0:T(8,128)(2,1)} %bitcast.141), calls=%async_computation | async-start | bytes 2949120 | tf_op jit(solution)/shard_map/all_to_all | solution.py:172
  28.4 5.2 %copy-start.17 = (f32[8]{0:T(128)S(1)}, f32[8]{0:T(128)}, u32[]{:S(2)}) copy-start(f32[8]{0:T(128)} %param.12) | copy-start | bytes 100
  33.7 2.1 copy-start.10
  38.9 24.2 %all-to-all-start.1 = ((bf16[32,2,24,256]{3,1,2,0:T(2,128)(2,1)}), bf16[32,2,24,256]{3,1,2,0:T(2,128)(2,1)}, u32[]{:S(2)}, u32[]{:S(2)}) async-start(bf16[32,2,24,256]{3,1,2,0:T(2,128)(2,1)} %bitcast.146), calls=%async_computation.1 | async-start | bytes 1572864 | tf_op jit(solution)/shard_map/all_to_all | solution.py:180
  45.0 143.8 %all-gather.2.cloned.1.call-start = ((), (), s32[]{:S(2)}) async-start(), calls=%async_computation.3 | async-start | bytes 3932160 | tf_op jit(solution)/shard_map/all_gather | solution.py:186
  104.3 2.6 %collective-permute-start = (bf16[8,1,256]{2,0,1:T(8,128)(2,1)S(1)}, bf16[8,1,256]{2,0,1:T(8,128)(2,1)S(1)}, u32[]{:S(2)}, u32[]{:S(2)}) collective-permute-start(bf16[8,1,256]{2,0,1:T(8,128)(2,1)S(1)} %copy.78), channel_id=1, source_target_pairs={{0,1},{1,2},{2,3},{3,0},{4,5},{5,6},{6,7},{7,4},{8,9},{9,10},{10,1... | collective-permute-start | bytes 12296 | tf_op jit(solution)/shard_map/ppermute | solution.py:22
  106.2 4.2 %collective-permute-start.1 = (bf16[8,1,256]{2,0,1:T(8,128)(2,1)S(1)}, bf16[8,1,256]{2,0,1:T(8,128)(2,1)S(1)}, u32[]{:S(2)}, u32[]{:S(2)}) collective-permute-start(bf16[8,1,256]{2,0,1:T(8,128)(2,1)S(1)} %copy.79), channel_id=1, source_target_pairs={{1,0},{2,1},{3,2},{0,3},{5,4},{6,5},{7,6},{4,7},{9,8},{10,9},{11,1... | collective-permute-start | bytes 12296 | tf_op jit(solution)/shard_map/ppermute | solution.py:23
  110.9 36.1 %collective-permute-start.2 = (bf16[8,362,256]{2,0,1:T(8,128)(2,1)}, bf16[8,362,256]{2,0,1:T(8,128)(2,1)}, u32[]{:S(2)}, u32[]{:S(2)}) collective-permute-start(bf16[8,362,256]{2,0,1:T(8,128)(2,1)} %constant_dynamic-update-slice_fusion), channel_id=1, source_target_pairs={{0,4},{4,8},{8,12},{12,16},{16,20},{20,24},{24,28},{1,5},{5,9},{9,... | collective-permute-start | bytes 4448264 | tf_op jit(solution)/shard_map/ppermute | solution.py:22
  114.0 66.2 %collective-permute-start.3 = (bf16[8,362,256]{2,0,1:T(8,128)(2,1)}, bf16[8,362,256]{2,0,1:T(8,128)(2,1)}, u32[]{:S(2)}, u32[]{:S(2)}) collective-permute-start(bf16[8,362,256]{2,0,1:T(8,128)(2,1)} %constant_dynamic-update-slice_fusion), channel_id=1, source_target_pairs={{4,0},{8,4},{12,8},{16,12},{20,16},{24,20},{28,24},{5,1},{9,5},{13... | collective-permute-start | bytes 4448264 | tf_op jit(solution)/shard_map/ppermute | solution.py:23
  121.0 2.5 copy-start.18
  183.6 1.3 copy-start.4
  184.9 1.3 copy-start.6
  186.2 1.2 copy-start.8
  188.8 3.4 %copy-start.14 = (bf16[2,256,256]{2,1,0:T(8,128)(2,1)S(1)}, bf16[2,256,256]{2,1,0:T(8,128)(2,1)}, u32[]{:S(2)}) copy-start(bf16[2,256,256]{2,1,0:T(8,128)(2,1)} %param.16) | copy-start | bytes 786436
  192.2 1.1 copy-start.12
  192.2 2.1 copy-start.16
  195.7 1.0 copy-start.13
  197.3 1.4 copy-start.3
  198.6 1.4 copy-start.2
  198.6 1.8 copy-start.11
  204.4 1.4 copy-start.5
  205.8 1.4 copy-start.7
  207.2 1.4 copy-start.9
  209.5 38.2 %copy-start.1 = (bf16[3,8,3,8]{3,1,2,0:T(8,128)(2,1)S(1)}, bf16[3,8,3,8]{3,1,2,0:T(8,128)(2,1)}, u32[]{:S(2)}) copy-start(bf16[3,8,3,8]{3,1,2,0:T(8,128)(2,1)} %param.15) | copy-start | bytes 3460
Sparse Core Ops, SparseCore 0:
  103.6 29.9 all-gather.1

commit v3 on v2

--- a/solution.py
+++ b/solution.py
@@ -120,6 +120,273 @@
     return out.reshape(-1)[:size].reshape(values.shape)
 
 
+def spectral_kernel(
+    n_lat,
+    n_lon,
+    own_rows,
+    field_ref,
+    rim_ref,
+    cols_ref,
+    leg_ref,
+    q_ref,
+    halo_ref,
+    tab_ref,
+    slab,
+    table,
+    spec,
+    gram,
+    same,
+    msg,
+    recv,
+    grid,
+    back,
+    own_sem,
+    s_lon,
+    r_lon,
+    s_out,
+    r_out,
+    s_back,
+    r_back,
+    s_q,
+    r_q,
+    s_halo,
+    r_halo,
+):
+    f32 = jnp.float32
+    bf16 = jnp.bfloat16
+    lat = lax.axis_index("lat")
+    lon = lax.axis_index("lon")
+    n = n_lat * n_lon
+    me = lat * n_lon + lon
+    rows = msg.shape[1]
+    part = rows // own_rows
+    band = slab.shape[1]
+    lon_cols = band // own_rows
+    nlon = lon_cols * n_lon
+    greet_all(n, n_lon, me)
+
+    up = push(rim_ref, halo_ref.at[0], s_halo.at[0], r_halo.at[0], me + n_lon, n_lon)
+    down = push(rim_ref, halo_ref.at[1], s_halo.at[1], r_halo.at[1], me - n_lon, n_lon)
+
+    def to_lon(t):
+        src = field_ref.at[pl.ds(pl.multiple_of(t * band, 16), band)]
+        return push(src, slab.at[lon], s_lon.at[t], r_lon.at[lon], lat * n_lon + t, n_lon)
+
+    for step in range(n_lon - 1, 0, -1):
+        to_lon(lax.rem(lon + step, n_lon)).start()
+
+    @pl.when(lat < n_lat - 1)
+    def _():
+        up.start()
+
+    @pl.when(lat > 0)
+    def _():
+        down.start()
+
+    slab[lon] = field_ref[pl.ds(pl.multiple_of(lon * band, 16), band)]
+
+    chunk = 64
+
+    def tables(i, carry):
+        at = pl.ds(pl.multiple_of(i * chunk, chunk), chunk)
+        order = cols_ref[at, 0:1]
+        shift = cols_ref[at, 1:2]
+        j = lax.broadcasted_iota(jnp.int32, (chunk, lon_cols), 1).astype(f32)
+        for s in range(n_lon):
+            turn = (j + float(s * lon_cols)) * order + shift
+            turn = turn - jnp.round(turn * (1.0 / nlon)) * float(nlon)
+            x = (0.25 - jnp.abs(turn) * (1.0 / nlon)) * 6.283185307179586
+            y = x * x
+            p = -2.505210838544172e-8
+            for c in (2.7557319223985893e-6, -1.984126984126984e-4, 8.333333333333333e-3, -0.16666666666666666, 1.0):
+                p = p * y + c
+            table[s, at] = (p * x).astype(bf16)
+        return carry
+
+    lax.fori_loop(0, table.shape[1] // chunk, tables, 0)
+    tab_ref[...] = table[lon]
+
+    total = gram.shape[0]
+    block = same.shape[0]
+    kind = lax.rem(lax.broadcasted_iota(jnp.int32, (block, total), 0), part)
+    other = lax.rem(lax.broadcasted_iota(jnp.int32, (block, total), 1), part)
+    same[...] = jnp.where(kind == other, 1.0, 0.0)
+
+    def grams(i, carry):
+        at = pl.ds(pl.multiple_of(i * block, 16), block)
+        product = lax.dot_general(
+            leg_ref[at], leg_ref[...], (((1,), (1,)), ((), ())), preferred_element_type=f32
+        )
+        gram[at] = (product * same[...]).astype(bf16)
+        return carry
+
+    lax.fori_loop(0, total // block, grams, 0)
+
+    for step in range(n_lon):
+        s = lax.rem(lon + step, n_lon)
+        if step:
+            push(slab.at[s], slab.at[s], s_lon.at[s], r_lon.at[s], me, n_lon).wait_recv()
+        wide = slab[s].astype(f32)
+        for a in range(own_rows):
+            piece = wide[a * lon_cols : (a + 1) * lon_cols].astype(bf16)
+            term = jnp.dot(table[s], piece, preferred_element_type=f32)
+            if step:
+                term = term + spec[a]
+            if step == n_lon - 1:
+                term = term * cols_ref[:, 2 + a : 3 + a]
+            spec[a] = term
+
+    def message(d):
+        at = pl.ds(pl.multiple_of(d * part, 8), part)
+        return jnp.concatenate([spec[a, at] for a in range(own_rows)], axis=0).astype(bf16)
+
+    def to_owner(d):
+        return push(msg.at[d], recv.at[me], s_out.at[d], r_out.at[me], d, n_lon)
+
+    def send_out(step, carry):
+        d = lax.rem(me + step, n)
+        msg[d] = message(d)
+        to_owner(d).start()
+        return carry
+
+    lax.fori_loop(1, n, send_out, 0)
+    recv[me] = message(me)
+
+    def await_out(step, carry):
+        d = lax.rem(me + n - step, n)
+        push(msg.at[d], recv.at[d], s_out.at[d], r_out.at[d], d, n_lon).wait_recv()
+        return carry
+
+    lax.fori_loop(1, n, await_out, 0)
+
+    per = block // rows
+    blocks = total // block
+
+    def to_rows(d):
+        return push(grid.at[d], back.at[me], s_back.at[d], r_back.at[me], d, n_lon)
+
+    def send_back(i, carry):
+        b = lax.rem(me // per + 1 + i, blocks)
+        at = pl.ds(pl.multiple_of(b * block, 16), block)
+        value = jnp.dot(
+            gram[at], recv[...].reshape(total, recv.shape[2]), preferred_element_type=f32
+        ).astype(bf16)
+        for e in range(per):
+            d = b * per + e
+            grid[d] = value[e * rows : (e + 1) * rows]
+
+            @pl.when(d != me)
+            def _():
+                to_rows(d).start()
+
+        return carry
+
+    lax.fori_loop(0, blocks, send_back, 0)
+    back[me] = grid[me]
+
+    def await_back(step, carry):
+        d = lax.rem(me + n - step, n)
+        push(grid.at[d], back.at[d], s_back.at[d], r_back.at[d], d, n_lon).wait_recv()
+        return carry
+
+    lax.fori_loop(1, n, await_back, 0)
+
+    def to_slab(t):
+        return push(back, q_ref.at[lon], s_q.at[t], r_q.at[lon], lat * n_lon + t, n_lon)
+
+    keep = pltpu.make_async_copy(back, q_ref.at[lon], own_sem)
+    keep.start()
+    half = n_lon // 2
+    side = lax.rem(lon, half)
+    cross = lax.rem(lon + half, n_lon)
+    if n_lon == 4:
+        mate = lon - side + (1 - side)
+        far = lax.rem(mate + half, n_lon)
+        to_slab(cross).start()
+        to_slab(mate).start()
+        push(back, q_ref.at[cross], s_q.at[cross], r_q.at[cross], me, n_lon).wait_recv()
+        relay = push(
+            q_ref.at[cross], q_ref.at[cross], s_q.at[far], r_q.at[n_lon], lat * n_lon + mate, n_lon
+        )
+        relay.start()
+        push(back, q_ref.at[mate], s_q.at[mate], r_q.at[mate], me, n_lon).wait_recv()
+        push(back, q_ref.at[far], s_q.at[far], r_q.at[n_lon], me, n_lon).wait_recv()
+        to_slab(cross).wait_send()
+        to_slab(mate).wait_send()
+        relay.wait_send()
+    else:
+        for step in range(1, n_lon):
+            to_slab(lax.rem(lon + step, n_lon)).start()
+        for step in range(1, n_lon):
+            t = lax.rem(lon + step, n_lon)
+            push(back, q_ref.at[t], s_q.at[t], r_q.at[t], me, n_lon).wait_recv()
+            to_slab(t).wait_send()
+    keep.wait()
+
+    for step in range(1, n_lon):
+        to_lon(lax.rem(lon + step, n_lon)).wait_send()
+
+    def drain(step, carry):
+        d = lax.rem(me + step, n)
+        to_owner(d).wait_send()
+        to_rows(d).wait_send()
+        return carry
+
+    lax.fori_loop(1, n, drain, 0)
+
+    @pl.when(lat < n_lat - 1)
+    def _():
+        up.wait_send()
+        down.wait_recv()
+
+    @pl.when(lat > 0)
+    def _():
+        down.wait_send()
+        up.wait_recv()
+
+
+def spectral(field, rimmed, cols, leg, n_lat, n_lon, own_rows):
+    lat_rows, lon_cols, channels = field.shape
+    n = n_lat * n_lon
+    total = leg.shape[0]
+    rows = total // n
+    bf16 = jnp.bfloat16
+    f32 = jnp.float32
+    band = own_rows * lon_cols
+    q_rows = cols.shape[0]
+    block = total // 8
+    vmem = pl.BlockSpec(memory_space=pltpu.VMEM)
+    anywhere = pl.BlockSpec(memory_space=pl.ANY)
+    dma = pltpu.SemaphoreType.DMA
+    flat_rim = rimmed.reshape(-1, channels)
+    return pl.pallas_call(
+        functools.partial(spectral_kernel, n_lat, n_lon, own_rows),
+        out_shape=(
+            jax.ShapeDtypeStruct((n_lon, n, rows, channels), bf16),
+            jax.ShapeDtypeStruct((2,) + flat_rim.shape, bf16),
+            jax.ShapeDtypeStruct((q_rows, lon_cols), bf16),
+        ),
+        in_specs=[vmem, anywhere, vmem, vmem],
+        out_specs=(anywhere, anywhere, vmem),
+        scratch_shapes=[
+            pltpu.VMEM((n_lon, band, channels), bf16),
+            pltpu.VMEM((n_lon, q_rows, lon_cols), bf16),
+            pltpu.VMEM((own_rows, q_rows, channels), f32),
+            pltpu.VMEM((total, total), bf16),
+            pltpu.VMEM((block, total), f32),
+        ]
+        + [pltpu.VMEM((n, rows, channels), bf16)] * 4
+        + [dma]
+        + [dma((n_lon,))] * 2
+        + [dma((n,))] * 4
+        + [dma((n_lon,)), dma((n_lon + 1,))]
+        + [dma((2,))] * 2,
+        compiler_params=pltpu.CompilerParams(
+            collective_id=1, has_side_effects=True, vmem_limit_bytes=52 * 2**20
+        ),
+    )(field.reshape(-1, channels), flat_rim, cols, leg)
+
+
 def outer_sum(left, right):
     return lax.dot_general(
         left, right, (((0,), (0,)), ((), ())), preferred_element_type=jnp.float32
@@ -153,50 +420,81 @@
     orders = order_slots.reshape(-1, slots_dev)
     orders = jnp.pad(orders, ((0, 0), (0, pad))).reshape(n_dev, own)
     flat_orders = orders.reshape(-1)
-    column = jnp.arange(nlon, dtype=jnp.int32)
-    phase = column[:, None] * flat_orders[None, :] % nlon
-    angle = phase.astype(f32) * (2.0 * jnp.pi / nlon)
-    cosine = jnp.cos(angle).astype(bf16).reshape(nlon, n_dev, own)
-    sine = (-jnp.sin(angle)).astype(bf16).reshape(nlon, n_dev, own)
-    table = jnp.stack([cosine, sine], axis=2)
-    factor = jnp.where(flat_orders == 0, 1.0, 2.0).astype(bf16).reshape(n_dev, own)
-
     own_leg = jnp.pad(legendre, ((0, pad), (0, 0), (0, 0)))
     own_leg = lax.dynamic_slice_in_dim(own_leg, lon_pos * own, own)
     own_orders = lax.dynamic_slice_in_dim(orders, lat_pos * n_lon + lon_pos, 1)[0]
     mask = jnp.arange(degrees, dtype=jnp.int32)[None, :] >= own_orders[:, None]
     masked = jnp.where(mask[:, None, :], own_leg, jnp.zeros((), bf16))
-    gram = jnp.einsum("kal,kbl->kab", own_leg, masked, preferred_element_type=f32).astype(bf16)
-
-    parts = field.reshape(n_lon, own_rows, lon_cols, channels)
-    slabs = lax.all_to_all(parts, "lon", split_axis=0, concat_axis=0, tiled=True)
-    slabs = slabs.transpose(1, 0, 2, 3).reshape(own_rows, nlon, channels)
     own_quad = lax.dynamic_slice_in_dim(quad_weight, lon_pos * own_rows, own_rows)
-    spectrum = jnp.einsum(
-        "ajc,jq->aqc", slabs, table.reshape(nlon, -1), preferred_element_type=f32
-    )
-    spectrum = (spectrum * (own_quad * (1.0 / nlon))[:, None, None]).astype(bf16)
-    spectrum = spectrum.reshape(own_rows, n_dev, 2 * own, channels).transpose(1, 0, 2, 3)
-    gathered = lax.all_to_all(spectrum, BOTH, split_axis=0, concat_axis=0, tiled=True)
-    gathered = gathered.reshape(nlat, 2, own, channels)
-    grid = jnp.einsum("kab,brkc->arkc", gram, gathered, preferred_element_type=f32).astype(bf16)
-    grid = grid.reshape(n_dev, own_rows, 2 * own, channels)
-    grid = lax.all_to_all(grid, BOTH, split_axis=0, concat_axis=0, tiled=True)
-    grid = grid.transpose(1, 0, 2, 3).reshape(own_rows, n_dev * 2 * own, channels)
-    grid = lax.all_gather(grid, "lon", axis=0, tiled=True)
-
-    here = lax.dynamic_slice_in_dim(table, lon_pos * lon_cols, lon_cols)
-    here = here * factor[None, :, None, :]
-    turned = jnp.stack([here[:, :, 1], -here[:, :, 0]], axis=2)
-    direct = here.reshape(lon_cols, -1)
-    turned = turned.reshape(lon_cols, -1)
-    waves = [
-        jnp.einsum("jq,aqc->ajc", piece, grid, preferred_element_type=f32).astype(bf16)
-        for piece in (direct, turned)
-    ]
-
     rimmed = padded(field, (("lon", 1),), 1, True)
-    extended = padded(rimmed, (("lat", 0),), lat_rows, False)
+    if own % 4 == 0 and n_dev * own % 64 == 0 and own_rows * lon_cols % 16 == 0:
+        shape = (n_dev, 2, own)
+        factor = jnp.where(orders == 0, 1.0, 2.0)[:, None, :] / nlon
+        cols = [
+            jnp.broadcast_to(orders[:, None, :].astype(f32), shape),
+            jnp.broadcast_to(jnp.array([0.0, nlon / 4], f32)[None, :, None], shape),
+        ]
+        cols += [jnp.broadcast_to(factor * own_quad[a], shape) for a in range(own_rows)]
+        cols = jnp.stack([c.reshape(-1) for c in cols], axis=1)
+        leg = jnp.broadcast_to(
+            masked.transpose(1, 0, 2)[:, None], (nlat, 2, own, degrees)
+        ).reshape(-1, degrees)
+        grid, halo, direct = spectral(field, rimmed, cols, leg, lax.axis_size("lat"), n_lon, own_rows)
+        grid = grid.reshape(n_lon, n_dev, own_rows, 2 * own, channels)
+        grid = grid.transpose(0, 2, 1, 3, 4).reshape(lat_rows, -1, channels)
+        pair = direct.reshape(n_dev, 2, own, lon_cols)
+        turned = jnp.stack([pair[:, 1], -pair[:, 0]], axis=1).reshape(-1, lon_cols)
+        waves = [
+            jnp.einsum("qj,aqc->ajc", piece, grid, preferred_element_type=f32).astype(bf16)
+            for piece in (direct, turned)
+        ]
+        halo = halo.reshape(2, lat_rows, lon_cols + 2, channels)
+        zero = jnp.zeros((), bf16)
+        extended = jnp.concatenate(
+            [
+                jnp.where(lat_pos > 0, halo[0], zero),
+                rimmed,
+                jnp.where(lat_pos < lax.axis_size("lat") - 1, halo[1], zero),
+            ],
+            axis=0,
+        )
+    else:
+        column = jnp.arange(nlon, dtype=jnp.int32)
+        phase = column[:, None] * flat_orders[None, :] % nlon
+        angle = phase.astype(f32) * (2.0 * jnp.pi / nlon)
+        cosine = jnp.cos(angle).astype(bf16).reshape(nlon, n_dev, own)
+        sine = (-jnp.sin(angle)).astype(bf16).reshape(nlon, n_dev, own)
+        table = jnp.stack([cosine, sine], axis=2)
+        factor = jnp.where(flat_orders == 0, 1.0, 2.0).astype(bf16).reshape(n_dev, own)
+        gram = jnp.einsum("kal,kbl->kab", own_leg, masked, preferred_element_type=f32).astype(bf16)
+
+        parts = field.reshape(n_lon, own_rows, lon_cols, channels)
+        slabs = lax.all_to_all(parts, "lon", split_axis=0, concat_axis=0, tiled=True)
+        slabs = slabs.transpose(1, 0, 2, 3).reshape(own_rows, nlon, channels)
+        spectrum = jnp.einsum(
+            "ajc,jq->aqc", slabs, table.reshape(nlon, -1), preferred_element_type=f32
+        )
+        spectrum = (spectrum * (own_quad * (1.0 / nlon))[:, None, None]).astype(bf16)
+        spectrum = spectrum.reshape(own_rows, n_dev, 2 * own, channels).transpose(1, 0, 2, 3)
+        gathered = lax.all_to_all(spectrum, BOTH, split_axis=0, concat_axis=0, tiled=True)
+        gathered = gathered.reshape(nlat, 2, own, channels)
+        grid = jnp.einsum("kab,brkc->arkc", gram, gathered, preferred_element_type=f32).astype(bf16)
+        grid = grid.reshape(n_dev, own_rows, 2 * own, channels)
+        grid = lax.all_to_all(grid, BOTH, split_axis=0, concat_axis=0, tiled=True)
+        grid = grid.transpose(1, 0, 2, 3).reshape(own_rows, n_dev * 2 * own, channels)
+        grid = lax.all_gather(grid, "lon", axis=0, tiled=True)
+
+        here = lax.dynamic_slice_in_dim(table, lon_pos * lon_cols, lon_cols)
+        here = here * factor[None, :, None, :]
+        turned = jnp.stack([here[:, :, 1], -here[:, :, 0]], axis=2)
+        direct = here.reshape(lon_cols, -1)
+        turned = turned.reshape(lon_cols, -1)
+        waves = [
+            jnp.einsum("jq,aqc->ajc", piece, grid, preferred_element_type=f32).astype(bf16)
+            for piece in (direct, turned)
+        ]
+        extended = padded(rimmed, (("lat", 0),), lat_rows, False)
+
     picks = support_blocks[0] - lat_pos + 1
     onehot = (picks[:, None] == jnp.arange(3, dtype=jnp.int32)[None, :]).astype(f32)
     operator = (

time: 256 us -> 218 us (0.85)
  Pallas kernels: 36 us -> 160 us
  waiting for transfers between devices: 75 us -> 0.01 us
  blocking collectives: 24 us -> 0 us
  starting transfers between devices: 19.5 us -> 1.83 us
  other arithmetic: 24.7 us -> 7.36 us
  local copies, waits for them, and re-layouts: 42.5 us -> 29.2 us
  between operations: 14.4 us -> 2.38 us
    pallas_call x0 -> x1, Pallas kernels: none -> 123 us  [spectral(): pl.pallas_call(functools.partial(spectral_kernel, n_lat, n_lon, own_rows)...]
    ppermute x2 -> x1, waiting for transfers between devices: 33.2 us -> 0.01 us  [padded(): after = lax.ppermute(leading, axis, down)]
    all_to_all x1 -> x0, blocking collectives: 24 us -> none  [local(): grid = lax.all_to_all(grid, BOTH, split_axis=0, concat_axis=0, tiled=True)]
    ppermute x2 -> x1, waiting for transfers between devices: 23.8 us -> 0.01 us  [padded(): before = lax.ppermute(last, axis, up)]
    all_to_all x2 -> x0, waiting for transfers between devices: 18 us -> none  [the longest x1 18 us: local(): lax.all_to_all(spectrum, BOTH, split_axis=0, concat_axis=0, tiled=True)]
    convert_element_type x2 -> x1, other arithmetic: 13.9 us -> 0.01 us  [local(): orders[:, None, :].astype(f32)]
    reshape x8 -> x4, local copies, waits for them, and re-layouts: 18.6 us -> 5.13 us  [the longest x1 3.32 us: local(): leg = jnp.broadcast_to(masked.transpose(1, 0, 2)[:, None], (nlat, 2, own,...]
    all_to_all x2 -> x0, starting transfers between devices: 11.2 us -> none  [the longest x1 6.09 us: local(): lax.all_to_all(spectrum, BOTH, split_axis=0, concat_axis=0, tiled=True)]
  transfers between devices with their start and end apart: 7 -> 2, of which waited for: 4 -> 0; matrix products, arithmetic and copies ran while one was open for 16% -> 5% of each run, Pallas kernels for 0% -> 0%
where the time goes in v3:
time: 218 us; the launch traced here: 217 us
  Pallas kernels  160 us (73%)
  local copies, waits for them, and re-layouts  29.2 us (13%)
  matrix products  16.4 us (8%)
  other arithmetic  7.36 us (3%)
  between operations  2.38 us (1%)
    pallas_call x1, Pallas kernels, spectral(): pl.pallas_call(functools.partial(spectral_kernel, n_lat, n_lon, own_rows)...  123 us
    pallas_call x1, Pallas kernels, reduce_all(): pl.pallas_call(functools.partial(reduce_kernel, n, n_lon), out_shape=jax....  36.8 us
    dot_general x2, matrix products, local(): jnp.einsum('qj,aqc->ajc', piece, grid, preferred_element_type=f32)  7 us
    unnamed x32, local copies, waits for them, and re-layouts  6.31 us
  transfers between devices with their start and end apart: 2, of which 0 were waited for; matrix products, arithmetic and copies ran while one was open for 5% of the time, Pallas kernels for 0%

profile of v3, /device:TPU:25, one launch (start us, length us, event | category | flops | bytes accessed | tf_op | source)
XLA Modules:
  0.0 217.1 jit_solution(6240281989468180255)
XLA Ops:
  0.6 0.8 fusion.74
  1.5 1.8 collective-permute-start
  3.3 0.7 add_bitcast_fusion
  3.9 0.7 dynamic_slice.9
  6.6 0.8 broadcast_in_dim_reshape.3
  8.1 0.7 broadcast_in_dim.58
  8.9 1.2 select_bitcast_fusion
  10.9 1.3 broadcast_in_dim.65
  12.2 3.3 %reshape.130.leg_ref = bf16[1536,384]{1,0:T(8,128)(2,1)} reshape(bf16[64,2,12,384]{3,2,1,0:T(8,128)(2,1)} %broadcast_in_dim.65) | data formatting | bytes 2359296 | tf_op jit(solution)/shard_map/reshape | solution.py:441
  15.9 1.1 copy-done.4
  17.3 1.3 reshape.129.rim_ref
  18.7 123.2 %shard_map.121 = (bf16[4,32,48,256]{3,2,1,0:T(8,128)(2,1)}, bf16[2,2896,256]{2,1,0:T(8,128)(2,1)}, bf16[768,360]{1,0:T(8,128)(2,1)S(1)}) custom-call(bf16[2880,256]{1,0:T(8,128)(2,1)} %bitcast.112, bf16[2896,256]{1,0:T(8,128)(2,1)} %reshape.129.rim_ref, f32[768,4]{1,0:T(8,128)S(1)} %copy.53.cols_ref, bf16[1536,384]{1,0:T(8,128)(2,1)} %reshape.130.leg_ref), custom_call_target="tpu_custom_call" | custom-call | tf_op jit(solution)/shard_map/pallas_call | solution.py:362
  141.9 3.8 %copy.54 = bf16[4,2,32,24,256]{4,3,2,1,0:T(8,128)(2,1)} copy(bf16[4,2,32,24,256]{4,3,1,2,0:T(8,128)(2,1)} %bitcast.119) | data formatting | bytes 6291456 | tf_op jit(solution)/shard_map/transpose | solution.py:444
  146.4 4.5 %convolution_convert_fusion.1 = bf16[8,256,360]{1,2,0:T(8,128)(2,1)} fusion(bf16[8,768,256]{2,1,0:T(8,128)(2,1)} %bitcast.117, bf16[768,360]{1,0:T(8,128)(2,1)S(1)} %get-tuple-element.7), kind=kOutput, calls=%fused_computation.27 | convolution fusion | flops 1133199360 | bytes 5173248 | tf_op jit(solution)/shard_map/qj,aqc->ajc/dot_general | solution.py:448
  150.9 2.5 %convolution_convert_fusion = bf16[8,256,360]{1,2,0:T(8,128)(2,1)} fusion(bf16[8,768,256]{2,1,0:T(8,128)(2,1)S(1)} %bitcast.118, bf16[768,360]{1,0:T(8,128)(2,1)S(1)} %reshape.135), kind=kOutput, calls=%fused_computation.26 | convolution fusion | flops 1133199360 | bytes 5173248 | tf_op jit(solution)/shard_map/qj,aqc->ajc/dot_general | solution.py:448
  153.4 1.3 slice_select_fusion.1
  154.7 1.5 select_n.51
  156.3 1.7 copy.58
  158.9 0.8 copy-done.5
  160.7 1.0 fusion.22
  161.7 1.0 fusion.19
  162.7 1.0 fusion.16
  164.6 1.0 copy-done.11
  166.2 0.8 copy-done.9
  169.8 0.8 copy-done.3
  171.0 3.4 %fusion.8 = (bf16[8,360,256]{2,1,0:T(8,128)(2,1)S(1)}, bf16[8,360,256]{2,1,0:T(8,128)(2,1)}) fusion(bf16[8,360,256]{2,1,0:T(8,128)(2,1)S(1)} %copy-done.10, f32[8,360,256]{2,1,0:T(8,128)S(1)} %bitcast.113, bf16[8,360,256]{2,1,0:T(8,128)(2,1)S(1)} %copy-done.3), kind=kLoop, calls=%fused_computation.17 | loop fusion | flops 18432000 | bytes 8847360 | tf_op jit(solution)/shard_map/convert_element_type | solution.py:521
  175.6 0.8 fusion.48
  176.4 0.8 fusion.50
  177.2 0.8 fusion.52
  178.1 36.8 %shard_map.122 = f32[32,80,128]{2,1,0:T(8,128)S(1)} custom-call(bf16[32,80,128]{2,1,0:T(8,128)(2,1)S(1)} %convert_element_type.67.x_ref), custom_call_target="tpu_custom_call" | custom-call | tf_op jit(solution)/shard_map/pallas_call | solution.py:102
  215.3 0.8 slice.99
  216.2 0.9 slice.100
  (72 shorter events, 11.9 us)
Async XLA Ops:
  0.6 7.3 %copy-start = (bf16[3,8,3,8]{3,1,2,0:T(8,128)(2,1)S(1)}, bf16[3,8,3,8]{3,1,2,0:T(8,128)(2,1)}, u32[]{:S(2)}) copy-start(bf16[3,8,3,8]{3,1,2,0:T(8,128)(2,1)} %param.16) | copy-start | bytes 3460
  1.5 14.1 %collective-permute-start = (bf16[8,1,256]{2,0,1:T(8,128)(2,1)S(1)}, bf16[8,1,256]{2,0,1:T(8,128)(2,1)S(1)}, u32[]{:S(2)}, u32[]{:S(2)}) collective-permute-start(bf16[8,1,256]{2,0,1:T(8,128)(2,1)S(1)} %copy.80), channel_id=1, source_target_pairs={{0,1},{1,2},{2,3},{3,0},{4,5},{5,6},{6,7},{7,4},{8,9},{9,10},{10,1... | collective-permute-start | bytes 12296 | tf_op jit(solution)/shard_map/ppermute | solution.py:22
  3.3 12.6 %collective-permute-start.1 = (bf16[8,1,256]{2,0,1:T(8,128)(2,1)S(1)}, bf16[8,1,256]{2,0,1:T(8,128)(2,1)S(1)}, u32[]{:S(2)}, u32[]{:S(2)}) collective-permute-start(bf16[8,1,256]{2,0,1:T(8,128)(2,1)S(1)} %copy.81), channel_id=1, source_target_pairs={{1,0},{2,1},{3,2},{0,3},{5,4},{6,5},{7,6},{4,7},{9,8},{10,9},{11,1... | collective-permute-start | bytes 12296 | tf_op jit(solution)/shard_map/ppermute | solution.py:23
  12.2 3.3 %copy-start.2 = (bf16[8,360,256]{2,1,0:T(8,128)(2,1)S(1)}, bf16[8,360,256]{2,1,0:T(8,128)(2,1)}, u32[]{:S(2)}) copy-start(bf16[8,360,256]{2,1,0:T(8,128)(2,1)} %param.10) | copy-start | bytes 4423684
  15.9 1.1 copy-start.4
  146.4 4.5 %copy-start.7 = (bf16[4,2,32,24,256]{4,3,2,1,0:T(8,128)(2,1)S(1)}, bf16[4,2,32,24,256]{4,3,2,1,0:T(8,128)(2,1)}, u32[]{:S(2)}) copy-start(bf16[4,2,32,24,256]{4,3,2,1,0:T(8,128)(2,1)} %copy.54) | copy-start | bytes 9437188
  150.9 2.5 %copy-start.8 = (bf16[2,2896,256]{2,1,0:T(8,128)(2,1)S(1)}, bf16[2,2896,256]{2,1,0:T(8,128)(2,1)}, u32[]{:S(2)}) copy-start(bf16[2,2896,256]{2,1,0:T(8,128)(2,1)} %get-tuple-element.8) | copy-start | bytes 8896516
  158.4 1.4 copy-start.5
  158.4 1.8 copy-start.6
  164.3 1.4 copy-start.11
  164.3 1.4 copy-start.13
  165.6 1.4 copy-start.9
  167.0 1.0 copy-start.12
  169.2 1.4 copy-start.3
  169.2 1.8 copy-start.10
  215.0 2.1 copy-start.1

commit v4 on v3

--- a/solution.py
+++ b/solution.py
@@ -50,69 +50,117 @@
     )
 
 
-def reduce_kernel(n, n_lon, x_ref, out_ref, parts, total, gath, s1, r1, s2, r2):
-    me = lax.axis_index("lat") * n_lon + lax.axis_index("lon")
-    greet_all(n, n_lon, me)
+def reduce_kernel(
+    n_lat, n_lon, x_ref, out_ref, half, pair, parts, total, gath, s0, r0, s1, r1, s2, r2, s3, r3
+):
+    f32 = jnp.float32
+    lat = lax.axis_index("lat")
+    lon = lax.axis_index("lon")
+    side = lax.rem(lon, 2)
+    mate = lon + 1 - 2 * side
+    wide = n_lon // 2
+    n = n_lat * wide
+    me = lat * wide + lon // 2
+
+    def place(g):
+        return (g // wide, lax.rem(g, wide) * 2 + side)
+
+    barrier = pltpu.get_barrier_semaphore()
+    pl.semaphore_signal(barrier, inc=1, device_id=(lat, mate), device_id_type=MESH)
+
+    def signal(step, carry):
+        pl.semaphore_signal(
+            barrier, inc=1, device_id=place(lax.rem(me + step, n)), device_id_type=MESH
+        )
+        return carry
+
+    lax.fori_loop(1, n, signal, 0)
+    pl.semaphore_wait(barrier, n)
+
+    def copy(src, dst, send_sem, recv_sem, where):
+        return pltpu.make_async_remote_copy(
+            src_ref=src,
+            dst_ref=dst,
+            send_sem=send_sem,
+            recv_sem=recv_sem,
+            device_id=where,
+            device_id_type=MESH,
+        )
+
+    first = copy(x_ref.at[1 - side], half, s0, r0, (lat, mate))
+    first.start()
+    first.wait()
 
     def scatter(step, carry):
-        d = lax.rem(me + step, n)
-        push(x_ref.at[d], parts.at[me], s1.at[d], r1.at[me], d, n_lon).start()
+        g = lax.rem(me + step, n)
+        pair[g] = (x_ref[side, g].astype(f32) + half[g].astype(f32)).astype(pair.dtype)
+        copy(pair.at[g], parts.at[me], s1.at[g], r1.at[me], place(g)).start()
         return carry
 
     lax.fori_loop(1, n, scatter, 0)
 
     def add(step, acc):
-        d = lax.rem(me + n - step, n)
-        push(x_ref.at[d], parts.at[d], s1.at[d], r1.at[d], d, n_lon).wait_recv()
-        return acc + parts[d].astype(jnp.float32)
-
-    total[...] = lax.fori_loop(1, n, add, x_ref[me].astype(jnp.float32)).astype(total.dtype)
+        g = lax.rem(me + n - step, n)
+        copy(pair.at[g], parts.at[g], s1.at[g], r1.at[g], place(g)).wait_recv()
+        return acc + parts[g].astype(f32)
+
+    own = x_ref[side, me].astype(f32) + half[me].astype(f32)
+    total[...] = lax.fori_loop(1, n, add, own).astype(total.dtype)
 
     def spread(step, carry):
-        d = lax.rem(me + step, n)
-        push(total, gath.at[me], s2.at[d], r2.at[me], d, n_lon).start()
+        g = lax.rem(me + step, n)
+        copy(total, gath.at[side, me], s2.at[g], r2.at[me], place(g)).start()
         return carry
 
     lax.fori_loop(1, n, spread, 0)
-    out_ref[me] = total[...].astype(out_ref.dtype)
+    gath[side, me] = total[...]
 
     def collect(step, carry):
-        d = lax.rem(me + n - step, n)
-        push(total, gath.at[d], s2.at[d], r2.at[d], d, n_lon).wait_recv()
-        out_ref[d] = gath[d].astype(out_ref.dtype)
+        g = lax.rem(me + n - step, n)
+        copy(total, gath.at[side, g], s2.at[g], r2.at[g], place(g)).wait_recv()
         return carry
 
     lax.fori_loop(1, n, collect, 0)
+    last = copy(gath.at[side], gath.at[side], s3, r3, (lat, mate))
+    last.start()
+    out_ref[side] = gath[side].astype(f32)
+    last.wait_send()
+    copy(gath.at[1 - side], gath.at[1 - side], s3, r3, (lat, mate)).wait_recv()
+    out_ref[1 - side] = gath[1 - side].astype(f32)
 
     def drain(step, carry):
-        d = lax.rem(me + step, n)
-        push(x_ref.at[d], parts.at[me], s1.at[d], r1.at[me], d, n_lon).wait_send()
-        push(total, gath.at[me], s2.at[d], r2.at[me], d, n_lon).wait_send()
+        g = lax.rem(me + step, n)
+        copy(pair.at[g], parts.at[me], s1.at[g], r1.at[me], place(g)).wait_send()
+        copy(total, gath.at[side, me], s2.at[g], r2.at[me], place(g)).wait_send()
         return carry
 
     lax.fori_loop(1, n, drain, 0)
 
 
-def reduce_all(values, n, n_lon):
+def reduce_all(values, n_lat, n_lon):
     size = values.size
-    rows = -(-size // (128 * n * 16)) * 16
-    flat = jnp.pad(values.reshape(-1), (0, rows * 128 * n - size)).reshape(n, rows, 128)
+    n = n_lat * n_lon // 2
+    rows = -(-size // (128 * 2 * n * 16)) * 16
+    flat = jnp.pad(values.reshape(-1), (0, rows * 256 * n - size)).reshape(2, n, rows, 128)
     vmem = pl.BlockSpec(memory_space=pltpu.VMEM)
-    dma = pltpu.SemaphoreType.DMA((n,))
+    dma = pltpu.SemaphoreType.DMA
+    slots = pltpu.VMEM((n, rows, 128), jnp.bfloat16)
     out = pl.pallas_call(
-        functools.partial(reduce_kernel, n, n_lon),
-        out_shape=jax.ShapeDtypeStruct((n, rows, 128), jnp.float32),
+        functools.partial(reduce_kernel, n_lat, n_lon),
+        out_shape=jax.ShapeDtypeStruct((2, n, rows, 128), jnp.float32),
         in_specs=[vmem],
         out_specs=vmem,
         scratch_shapes=[
-            pltpu.VMEM((n, rows, 128), jnp.bfloat16),
+            slots,
+            slots,
+            slots,
             pltpu.VMEM((rows, 128), jnp.bfloat16),
-            pltpu.VMEM((n, rows, 128), jnp.bfloat16),
+            pltpu.VMEM((2, n, rows, 128), jnp.bfloat16),
             dma,
             dma,
-            dma,
-            dma,
-        ],
+        ]
+        + [dma((n,))] * 4
+        + [dma, dma],
         compiler_params=pltpu.CompilerParams(
             collective_id=0, has_side_effects=True, vmem_limit_bytes=32 * 2**20
         ),
@@ -140,6 +188,8 @@
     recv,
     grid,
     back,
+    pack,
+    legs,
     own_sem,
     s_lon,
     r_lon,
@@ -165,8 +215,50 @@
     nlon = lon_cols * n_lon
     greet_all(n, n_lon, me)
 
-    up = push(rim_ref, halo_ref.at[0], s_halo.at[0], r_halo.at[0], me + n_lon, n_lon)
-    down = push(rim_ref, halo_ref.at[1], s_halo.at[1], r_halo.at[1], me - n_lon, n_lon)
+    odd = lax.rem(lat, 2)
+    sign = 1 - 2 * odd
+    hand_to = lat + 2 * sign
+    has_other = jnp.logical_and(hand_to >= 0, hand_to < n_lat)
+    from_other = lat - 2 * sign
+    gets_other = jnp.logical_and(from_other >= 0, from_other < n_lat)
+    cut = rim_ref.shape[0] // 32 * 16
+
+    def piece_of(c):
+        return pl.ds(cut, rim_ref.shape[0] - cut) if c else pl.ds(0, cut)
+
+    def to_mate(c):
+        at = piece_of(c)
+        return push(
+            rim_ref.at[at],
+            halo_ref.at[odd, at],
+            s_halo.at[c],
+            r_halo.at[c],
+            (lat + sign) * n_lon + lon,
+            n_lon,
+        )
+
+    def got_mate(c):
+        at = piece_of(c)
+        dst = halo_ref.at[1 - odd, at]
+        return push(dst, dst, s_halo.at[c], r_halo.at[c], me, n_lon)
+
+    def hand_on(c):
+        at = piece_of(c)
+        return push(
+            halo_ref.at[1 - odd, at],
+            halo_ref.at[odd, at],
+            s_halo.at[2 + c],
+            r_halo.at[2 + c],
+            hand_to * n_lon + lon,
+            n_lon,
+        )
+
+    def relay_halo(c):
+        got_mate(c).wait_recv()
+
+        @pl.when(has_other)
+        def _():
+            hand_on(c).start()
 
     def to_lon(t):
         src = field_ref.at[pl.ds(pl.multiple_of(t * band, 16), band)]
@@ -175,14 +267,7 @@
     for step in range(n_lon - 1, 0, -1):
         to_lon(lax.rem(lon + step, n_lon)).start()
 
-    @pl.when(lat < n_lat - 1)
-    def _():
-        up.start()
-
-    @pl.when(lat > 0)
-    def _():
-        down.start()
-
+    to_mate(0).start()
     slab[lon] = field_ref[pl.ds(pl.multiple_of(lon * band, 16), band)]
 
     chunk = 64
@@ -205,6 +290,8 @@
 
     lax.fori_loop(0, table.shape[1] // chunk, tables, 0)
     tab_ref[...] = table[lon]
+    relay_halo(0)
+    to_mate(1).start()
 
     total = gram.shape[0]
     block = same.shape[0]
@@ -212,10 +299,24 @@
     other = lax.rem(lax.broadcasted_iota(jnp.int32, (block, total), 1), part)
     same[...] = jnp.where(kind == other, 1.0, 0.0)
 
+    nlat = n_lat * own_rows * n_lon
+    own = part // 2
+
+    def spread_rows(i, carry):
+        at = pl.ds(pl.multiple_of(i * block, 16), block)
+        row = i * block + lax.broadcasted_iota(jnp.int32, (block, 1), 0)
+        wanted = lax.rem(row, own) * nlat + lax.div(row, part)
+        column = lax.broadcasted_iota(jnp.int32, (block, leg_ref.shape[0]), 1)
+        pick = jnp.where(column == wanted, 1.0, 0.0).astype(bf16)
+        legs[at] = jnp.dot(pick, leg_ref[...], preferred_element_type=f32).astype(bf16)
+        return carry
+
+    lax.fori_loop(0, total // block, spread_rows, 0)
+
     def grams(i, carry):
         at = pl.ds(pl.multiple_of(i * block, 16), block)
         product = lax.dot_general(
-            leg_ref[at], leg_ref[...], (((1,), (1,)), ((), ())), preferred_element_type=f32
+            legs[at], legs[...], (((1,), (1,)), ((), ())), preferred_element_type=f32
         )
         gram[at] = (product * same[...]).astype(bf16)
         return carry
@@ -291,10 +392,15 @@
 
     lax.fori_loop(1, n, await_back, 0)
 
+    relay_halo(1)
+    for a in range(own_rows):
+        wide = back[:, a * part : (a + 1) * part].astype(f32)
+        pack[a] = wide.reshape(pack.shape[1:]).astype(bf16)
+
     def to_slab(t):
-        return push(back, q_ref.at[lon], s_q.at[t], r_q.at[lon], lat * n_lon + t, n_lon)
-
-    keep = pltpu.make_async_copy(back, q_ref.at[lon], own_sem)
+        return push(pack, q_ref.at[lon], s_q.at[t], r_q.at[lon], lat * n_lon + t, n_lon)
+
+    keep = pltpu.make_async_copy(pack, q_ref.at[lon], own_sem)
     keep.start()
     half = n_lon // 2
     side = lax.rem(lon, half)
@@ -304,13 +410,13 @@
         far = lax.rem(mate + half, n_lon)
         to_slab(cross).start()
         to_slab(mate).start()
-        push(back, q_ref.at[cross], s_q.at[cross], r_q.at[cross], me, n_lon).wait_recv()
+        push(pack, q_ref.at[cross], s_q.at[cross], r_q.at[cross], me, n_lon).wait_recv()
         relay = push(
             q_ref.at[cross], q_ref.at[cross], s_q.at[far], r_q.at[n_lon], lat * n_lon + mate, n_lon
         )
         relay.start()
-        push(back, q_ref.at[mate], s_q.at[mate], r_q.at[mate], me, n_lon).wait_recv()
-        push(back, q_ref.at[far], s_q.at[far], r_q.at[n_lon], me, n_lon).wait_recv()
+        push(pack, q_ref.at[mate], s_q.at[mate], r_q.at[mate], me, n_lon).wait_recv()
+        push(pack, q_ref.at[far], s_q.at[far], r_q.at[n_lon], me, n_lon).wait_recv()
         to_slab(cross).wait_send()
         to_slab(mate).wait_send()
         relay.wait_send()
@@ -319,7 +425,7 @@
             to_slab(lax.rem(lon + step, n_lon)).start()
         for step in range(1, n_lon):
             t = lax.rem(lon + step, n_lon)
-            push(back, q_ref.at[t], s_q.at[t], r_q.at[t], me, n_lon).wait_recv()
+            push(pack, q_ref.at[t], s_q.at[t], r_q.at[t], me, n_lon).wait_recv()
             to_slab(t).wait_send()
     keep.wait()
 
@@ -334,21 +440,23 @@
 
     lax.fori_loop(1, n, drain, 0)
 
-    @pl.when(lat < n_lat - 1)
-    def _():
-        up.wait_send()
-        down.wait_recv()
-
-    @pl.when(lat > 0)
-    def _():
-        down.wait_send()
-        up.wait_recv()
+    for c in range(2):
+        to_mate(c).wait_send()
+
+        @pl.when(has_other)
+        def _():
+            hand_on(c).wait_send()
+
+        @pl.when(gets_other)
+        def _():
+            dst = halo_ref.at[odd, piece_of(c)]
+            push(dst, dst, s_halo.at[2 + c], r_halo.at[2 + c], me, n_lon).wait_recv()
 
 
 def spectral(field, rimmed, cols, leg, n_lat, n_lon, own_rows):
     lat_rows, lon_cols, channels = field.shape
     n = n_lat * n_lon
-    total = leg.shape[0]
+    total = 2 * leg.shape[0]
     rows = total // n
     bf16 = jnp.bfloat16
     f32 = jnp.float32
@@ -362,7 +470,7 @@
     return pl.pallas_call(
         functools.partial(spectral_kernel, n_lat, n_lon, own_rows),
         out_shape=(
-            jax.ShapeDtypeStruct((n_lon, n, rows, channels), bf16),
+            jax.ShapeDtypeStruct((n_lon, own_rows, q_rows, channels), bf16),
             jax.ShapeDtypeStruct((2,) + flat_rim.shape, bf16),
             jax.ShapeDtypeStruct((q_rows, lon_cols), bf16),
         ),
@@ -376,11 +484,12 @@
             pltpu.VMEM((block, total), f32),
         ]
         + [pltpu.VMEM((n, rows, channels), bf16)] * 4
+        + [pltpu.VMEM((own_rows, q_rows, channels), bf16), pltpu.VMEM((total, leg.shape[1]), bf16)]
         + [dma]
         + [dma((n_lon,))] * 2
         + [dma((n,))] * 4
         + [dma((n_lon,)), dma((n_lon + 1,))]
-        + [dma((2,))] * 2,
+        + [dma((4,))] * 2,
         compiler_params=pltpu.CompilerParams(
             collective_id=1, has_side_effects=True, vmem_limit_bytes=52 * 2**20
         ),
@@ -436,12 +545,9 @@
         ]
         cols += [jnp.broadcast_to(factor * own_quad[a], shape) for a in range(own_rows)]
         cols = jnp.stack([c.reshape(-1) for c in cols], axis=1)
-        leg = jnp.broadcast_to(
-            masked.transpose(1, 0, 2)[:, None], (nlat, 2, own, degrees)
-        ).reshape(-1, degrees)
+        leg = masked.reshape(-1, degrees)
         grid, halo, direct = spectral(field, rimmed, cols, leg, lax.axis_size("lat"), n_lon, own_rows)
-        grid = grid.reshape(n_lon, n_dev, own_rows, 2 * own, channels)
-        grid = grid.transpose(0, 2, 1, 3, 4).reshape(lat_rows, -1, channels)
+        grid = grid.reshape(lat_rows, -1, channels)
         pair = direct.reshape(n_dev, 2, own, lon_cols)
         turned = jnp.stack([pair[:, 1], -pair[:, 0]], axis=1).reshape(-1, lon_cols)
         waves = [
@@ -520,7 +626,7 @@
     (grad_pre,) = pullback(cotangent.astype(f32))
     flat_grad = grad_pre.astype(bf16).reshape(-1, channels)
     grads = jnp.concatenate([outer_sum(s, flat_grad) for s in sources], axis=0)
-    total = reduce_all(grads.reshape(5, channels, channels), n_dev, n_lon)
+    total = reduce_all(grads.reshape(5, channels, channels), lax.axis_size("lat"), n_lon)
     return (output, total[:2], total[2:])
 
 

time: 218 us -> 182 us (0.83)
  Pallas kernels: 160 us -> 126 us
  local copies, waits for them, and re-layouts: 29.2 us -> 24.4 us
  other arithmetic: 7.36 us -> 10.4 us
    pallas_call x1, Pallas kernels: 123 us -> 100 us  [spectral(): pl.pallas_call(functools.partial(spectral_kernel, n_lat, n_lon, own_rows)...]
    pallas_call x1, Pallas kernels: 36.8 us -> 26.2 us  [reduce_all(): pl.pallas_call(functools.partial(reduce_kernel, n_lat, n_lon), out_shape=...]
    transpose x2 -> x0, local copies, waits for them, and re-layouts: 4.13 us -> none  [the longest x1 3.77 us: local(): grid = grid.transpose(0, 2, 1, 3, 4).reshape(lat_rows, -1, channels)]
    reshape x1 -> x0, local copies, waits for them, and re-layouts: 3.32 us -> none  [local(): leg = jnp.broadcast_to(masked.transpose(1, 0, 2)[:, None], (nlat, 2, own,...]
    select_n x1, other arithmetic: 1.34 us -> 3.68 us  [local(): jnp.where(lat_pos > 0, halo[0], zero)]
    unnamed x32 -> x34, local copies, waits for them, and re-layouts: 6.31 us -> 7.78 us
  transfers between devices with their start and end apart: 2 -> 2, of which waited for: 0 -> 0; matrix products, arithmetic and copies ran while one was open for 5% -> 3% of each run, Pallas kernels for 0% -> 0%
where the time goes in v4:
time: 182 us; the launch traced here: 181 us
  Pallas kernels  126 us (69%)
  local copies, waits for them, and re-layouts  24.4 us (13%)
  matrix products  15.9 us (9%)
  other arithmetic  10.4 us (6%)
  between operations  2.43 us (1%)
  starting transfers between devices  1.83 us (1%)
    pallas_call x1, Pallas kernels, spectral(): pl.pallas_call(functools.partial(spectral_kernel, n_lat, n_lon, own_rows)...  100 us
    pallas_call x1, Pallas kernels, reduce_all(): pl.pallas_call(functools.partial(reduce_kernel, n_lat, n_lon), out_shape=...  26.2 us
    unnamed x34, local copies, waits for them, and re-layouts  7.78 us
    dot_general x2, matrix products, local(): jnp.einsum('qj,aqc->ajc', piece, grid, preferred_element_type=f32)  6.63 us
    select_n x1, other arithmetic, local(): jnp.where(lat_pos > 0, halo[0], zero)  3.68 us
  transfers between devices with their start and end apart: 2, of which 0 were waited for; matrix products, arithmetic and copies ran while one was open for 3% of the time, Pallas kernels for 0%

profile of v4, /device:TPU:25, one launch (start us, length us, event | category | flops | bytes accessed | tf_op | source)
XLA Modules:
  0.0 181.2 jit_solution(9525434489177485389)
XLA Ops:
  0.7 0.9 fusion.74
  1.6 1.8 %collective-permute-start = (bf16[8,1,256]{2,0,1:T(8,128)(2,1)S(1)}, bf16[8,1,256]{2,0,1:T(8,128)(2,1)S(1)}, u32[]{:S(2)}, u32[]{:S(2)}) collective-permute-start(bf16[8,1,256]{2,0,1:T(8,128)(2,1)S(1)} %copy.74), channel_id=1, source_target_pairs={{0,1},{1,2},{2,3},{3,0},{4,5},{5,6},{6,7},{7,4},{8,9},{9,10},{10,1... | collective-permute-start | bytes 12296 | tf_op jit(solution)/shard_map/ppermute | solution.py:22
  3.4 0.7 dynamic_slice.9
  4.7 0.8 broadcast_in_dim_reshape.3
  7.3 0.7 broadcast_in_dim.52
  9.0 1.2 dynamic-slice_select_fusion
  11.0 1.1 copy-done.5
  12.4 1.4 reshape.125.rim_ref
  13.8 100.0 %shard_map.121 = (bf16[4,2,768,256]{3,2,1,0:T(8,128)(2,1)}, bf16[2,2896,256]{2,1,0:T(8,128)(2,1)}, bf16[768,360]{1,0:T(8,128)(2,1)S(1)}) custom-call(bf16[2880,256]{1,0:T(8,128)(2,1)} %bitcast.113, bf16[2896,256]{1,0:T(8,128)(2,1)} %reshape.125.rim_ref, f32[768,4]{1,0:T(8,128)S(1)} %copy.48.cols_ref, bf16[768,384]{1,0:T(8,128)(2,1)S(1)} %bitcast.110), custom_call_target="tpu_custom_call" | custom-call | tf_op jit(solution)/shard_map/pallas_call | solution.py:470
  113.9 3.7 %slice_select_fusion.1 = (bf16[1,2896,256]{2,1,0:T(8,128)(2,1)}, bf16[1,2896,256]{2,1,0:T(8,128)(2,1)}) fusion(bf16[2,2896,256]{2,1,0:T(8,128)(2,1)} %get-tuple-element.8, pred[]{:T(512)S(6)} %gt.3, pred[]{:T(512)S(6)} %lt.15), kind=kLoop, calls=%fused_computation.32 | loop fusion | flops 1482752 | bytes 5931010 | tf_op jit(solution)/shard_map/jit(_where)/select_n | solution.py:561
  117.5 1.5 select_n.51
  119.1 1.6 copy.52
  120.7 1.5 select_n.54
  122.8 0.9 copy-done.6
  124.5 1.0 fusion.16
  125.4 1.1 copy-done.2
  126.8 0.9 copy-done.8
  127.9 1.0 pad_maximum_fusion.1
  129.0 1.6 reshape.130
  130.6 3.4 %convolution_convert_fusion.1 = bf16[8,256,360]{1,2,0:T(8,128)(2,1)S(1)} fusion(bf16[8,768,256]{2,1,0:T(8,128)(2,1)} %bitcast.120, bf16[768,360]{1,0:T(8,128)(2,1)S(1)} %get-tuple-element.7), kind=kOutput, calls=%fused_computation.27 | convolution fusion | flops 1133199360 | bytes 5173248 | tf_op jit(solution)/shard_map/qj,aqc->ajc/dot_general | solution.py:554
  134.0 3.2 %convolution_convert_fusion = bf16[8,256,360]{1,2,0:T(8,128)(2,1)S(1)} fusion(bf16[8,768,256]{2,1,0:T(8,128)(2,1)} %bitcast.121, bf16[768,360]{1,0:T(8,128)(2,1)S(1)} %reshape.130), kind=kOutput, calls=%fused_computation.26 | convolution fusion | flops 1133199360 | bytes 5173248 | tf_op jit(solution)/shard_map/qj,aqc->ajc/dot_general | solution.py:554
  137.3 0.9 fusion.19
  138.6 0.9 fusion.22
  143.7 0.8 copy-done.4
  145.0 3.4 %fusion.8 = (bf16[8,360,256]{2,1,0:T(8,128)(2,1)S(1)}, bf16[8,360,256]{2,1,0:T(8,128)(2,1)}) fusion(bf16[8,360,256]{2,1,0:T(8,128)(2,1)S(1)} %copy-done.10, f32[8,360,256]{2,1,0:T(8,128)S(1)} %bitcast.114, bf16[8,360,256]{2,1,0:T(8,128)(2,1)S(1)} %copy-done.4), kind=kLoop, calls=%fused_computation.17 | loop fusion | flops 18432000 | bytes 8847360 | tf_op jit(solution)/shard_map/convert_element_type | solution.py:627
  149.6 0.7 copy-done.9
  150.3 0.8 fusion.48
  151.1 0.8 fusion.50
  151.9 0.8 fusion.52
  152.8 26.2 %shard_map.122 = f32[2,16,80,128]{3,2,1,0:T(8,128)S(1)} custom-call(bf16[2,16,80,128]{3,2,1,0:T(8,128)(2,1)S(1)} %convert_element_type.67.x_ref), custom_call_target="tpu_custom_call" | custom-call | tf_op jit(solution)/shard_map/pallas_call | solution.py:148
  179.4 0.9 slice.100
  180.4 0.8 slice.99
  (71 shorter events, 11.6 us)
Async XLA Ops:
  0.6 8.3 %copy-start = (bf16[3,8,3,8]{3,1,2,0:T(8,128)(2,1)S(1)}, bf16[3,8,3,8]{3,1,2,0:T(8,128)(2,1)}, u32[]{:S(2)}) copy-start(bf16[3,8,3,8]{3,1,2,0:T(8,128)(2,1)} %param.16) | copy-start | bytes 3460
  0.6 10.0 %copy-start.3 = (bf16[8,360,256]{2,1,0:T(8,128)(2,1)S(1)}, bf16[8,360,256]{2,1,0:T(8,128)(2,1)}, u32[]{:S(2)}) copy-start(bf16[8,360,256]{2,1,0:T(8,128)(2,1)} %param.10) | copy-start | bytes 4423684
  1.6 9.1 %collective-permute-start = (bf16[8,1,256]{2,0,1:T(8,128)(2,1)S(1)}, bf16[8,1,256]{2,0,1:T(8,128)(2,1)S(1)}, u32[]{:S(2)}, u32[]{:S(2)}) collective-permute-start(bf16[8,1,256]{2,0,1:T(8,128)(2,1)S(1)} %copy.74), channel_id=1, source_target_pairs={{0,1},{1,2},{2,3},{3,0},{4,5},{5,6},{6,7},{7,4},{8,9},{9,10},{10,1... | collective-permute-start | bytes 12296 | tf_op jit(solution)/shard_map/ppermute | solution.py:22
  3.4 7.6 %collective-permute-start.1 = (bf16[8,1,256]{2,0,1:T(8,128)(2,1)S(1)}, bf16[8,1,256]{2,0,1:T(8,128)(2,1)S(1)}, u32[]{:S(2)}, u32[]{:S(2)}) collective-permute-start(bf16[8,1,256]{2,0,1:T(8,128)(2,1)S(1)} %copy.75), channel_id=1, source_target_pairs={{1,0},{2,1},{3,2},{0,3},{5,4},{6,5},{7,6},{4,7},{9,8},{10,9},{11,1... | collective-permute-start | bytes 12296 | tf_op jit(solution)/shard_map/ppermute | solution.py:23
  11.0 1.1 copy-start.5
  122.3 1.4 copy-start.6
  122.3 1.8 %copy-start.7 = (bf16[8,362,256]{2,0,1:T(8,128)(2,1)S(1)}, bf16[8,362,256]{2,0,1:T(8,128)(2,1)}, u32[]{:S(2)}) copy-start(bf16[8,362,256]{2,0,1:T(8,128)(2,1)} %copy.52) | copy-start | bytes 4448260
  124.4 2.0 %copy-start.2 = (bf16[24,362,256]{2,0,1:T(8,128)(2,1)}, bf16[24,362,256]{2,0,1:T(8,128)(2,1)S(1)}, u32[]{:S(2)}) copy-start(bf16[24,362,256]{2,0,1:T(8,128)(2,1)S(1)} %pad_maximum_fusion) | copy-start | bytes 13344772
  126.5 1.2 copy-start.8
  129.0 8.3 %slice-start = ((s8[4448256]{0:T(1024)(128)(4,1)}), s8[253952]{0:T(1024)(128)(4,1)S(1)}, s32[]{:S(2)}) async-start(s8[4448256]{0:T(1024)(128)(4,1)} %bitcast.111), calls=%async_computation | async-start | bytes 507904
  130.6 6.7 %slice-start.1 = ((s8[4448256]{0:T(1024)(128)(4,1)}), s8[4194304]{0:T(1024)(128)(4,1)S(1)}, s32[]{:S(2)}) async-start(s8[4448256]{0:T(1024)(128)(4,1)} %bitcast.111), calls=%async_computation.1 | async-start | bytes 8388608
  139.5 1.0 copy-start.12
  141.0 1.0 copy-start.11
  143.2 1.4 copy-start.4
  143.2 1.8 copy-start.10
  149.0 1.4 copy-start.9
  179.1 2.1 %copy-start.1 = (bf16[3,8,3,8]{3,1,2,0:T(8,128)(2,1)S(1)}, bf16[3,8,3,8]{3,1,2,0:T(8,128)(2,1)}, u32[]{:S(2)}) copy-start(bf16[3,8,3,8]{3,1,2,0:T(8,128)(2,1)} %param.16) | copy-start | bytes 3460

commit v5 on v4

--- a/solution.py
+++ b/solution.py
@@ -8,6 +8,7 @@
 from jax.sharding import PartitionSpec as P
 
 MESH = pl.DeviceIdType.MESH
+SINE = (2.7557319223985893e-6, -1.984126984126984e-4, 8.333333333333333e-3, -1 / 6, 1.0)
 
 BOTH = ("lat", "lon")
 
@@ -177,7 +178,7 @@
     cols_ref,
     leg_ref,
     q_ref,
-    halo_ref,
+    ext_ref,
     tab_ref,
     slab,
     table,
@@ -190,6 +191,7 @@
     back,
     pack,
     legs,
+    zeros,
     own_sem,
     s_lon,
     r_lon,
@@ -230,7 +232,7 @@
         at = piece_of(c)
         return push(
             rim_ref.at[at],
-            halo_ref.at[odd, at],
+            ext_ref.at[2 * odd, at],
             s_halo.at[c],
             r_halo.at[c],
             (lat + sign) * n_lon + lon,
@@ -239,14 +241,14 @@
 
     def got_mate(c):
         at = piece_of(c)
-        dst = halo_ref.at[1 - odd, at]
+        dst = ext_ref.at[2 - 2 * odd, at]
         return push(dst, dst, s_halo.at[c], r_halo.at[c], me, n_lon)
 
     def hand_on(c):
         at = piece_of(c)
         return push(
-            halo_ref.at[1 - odd, at],
-            halo_ref.at[odd, at],
+            ext_ref.at[2 - 2 * odd, at],
+            ext_ref.at[2 * odd, at],
             s_halo.at[2 + c],
             r_halo.at[2 + c],
             hand_to * n_lon + lon,
@@ -268,9 +270,27 @@
         to_lon(lax.rem(lon + step, n_lon)).start()
 
     to_mate(0).start()
+    own_block = pltpu.make_async_copy(rim_ref, ext_ref.at[1], own_sem.at[1])
+    own_block.start()
+    blank = pltpu.make_async_copy(zeros, ext_ref.at[2 * odd], own_sem.at[2])
+
+    @pl.when(jnp.logical_not(gets_other))
+    def _():
+        zeros[...] = jnp.zeros_like(zeros)
+        blank.start()
+
     slab[lon] = field_ref[pl.ds(pl.multiple_of(lon * band, 16), band)]
 
     chunk = 64
+
+    def wave(phase):
+        turn = phase - jnp.round(phase * (1.0 / nlon)) * float(nlon)
+        x = (0.25 - jnp.abs(turn) * (1.0 / nlon)) * 6.283185307179586
+        y = x * x
+        p = -2.505210838544172e-8
+        for c in SINE:
+            p = p * y + c
+        return (p * x).astype(bf16)
 
     def tables(i, carry):
         at = pl.ds(pl.multiple_of(i * chunk, chunk), chunk)
@@ -278,50 +298,14 @@
         shift = cols_ref[at, 1:2]
         j = lax.broadcasted_iota(jnp.int32, (chunk, lon_cols), 1).astype(f32)
         for s in range(n_lon):
-            turn = (j + float(s * lon_cols)) * order + shift
-            turn = turn - jnp.round(turn * (1.0 / nlon)) * float(nlon)
-            x = (0.25 - jnp.abs(turn) * (1.0 / nlon)) * 6.283185307179586
-            y = x * x
-            p = -2.505210838544172e-8
-            for c in (2.7557319223985893e-6, -1.984126984126984e-4, 8.333333333333333e-3, -0.16666666666666666, 1.0):
-                p = p * y + c
-            table[s, at] = (p * x).astype(bf16)
+            table[s, at] = wave((j + float(s * lon_cols)) * order + shift)
+        tab_ref[1, at] = wave((j + (lon * lon_cols).astype(f32)) * order + (shift + nlon / 4.0))
         return carry
 
     lax.fori_loop(0, table.shape[1] // chunk, tables, 0)
-    tab_ref[...] = table[lon]
+    tab_ref[0] = table[lon]
     relay_halo(0)
     to_mate(1).start()
-
-    total = gram.shape[0]
-    block = same.shape[0]
-    kind = lax.rem(lax.broadcasted_iota(jnp.int32, (block, total), 0), part)
-    other = lax.rem(lax.broadcasted_iota(jnp.int32, (block, total), 1), part)
-    same[...] = jnp.where(kind == other, 1.0, 0.0)
-
-    nlat = n_lat * own_rows * n_lon
-    own = part // 2
-
-    def spread_rows(i, carry):
-        at = pl.ds(pl.multiple_of(i * block, 16), block)
-        row = i * block + lax.broadcasted_iota(jnp.int32, (block, 1), 0)
-        wanted = lax.rem(row, own) * nlat + lax.div(row, part)
-        column = lax.broadcasted_iota(jnp.int32, (block, leg_ref.shape[0]), 1)
-        pick = jnp.where(column == wanted, 1.0, 0.0).astype(bf16)
-        legs[at] = jnp.dot(pick, leg_ref[...], preferred_element_type=f32).astype(bf16)
-        return carry
-
-    lax.fori_loop(0, total // block, spread_rows, 0)
-
-    def grams(i, carry):
-        at = pl.ds(pl.multiple_of(i * block, 16), block)
-        product = lax.dot_general(
-            legs[at], legs[...], (((1,), (1,)), ((), ())), preferred_element_type=f32
-        )
-        gram[at] = (product * same[...]).astype(bf16)
-        return carry
-
-    lax.fori_loop(0, total // block, grams, 0)
 
     for step in range(n_lon):
         s = lax.rem(lon + step, n_lon)
@@ -353,6 +337,36 @@
     lax.fori_loop(1, n, send_out, 0)
     recv[me] = message(me)
 
+    total = gram.shape[0]
+    block = same.shape[0]
+    kind = lax.rem(lax.broadcasted_iota(jnp.int32, (block, total), 0), part)
+    other = lax.rem(lax.broadcasted_iota(jnp.int32, (block, total), 1), part)
+    same[...] = jnp.where(kind == other, 1.0, 0.0)
+
+    nlat = n_lat * own_rows * n_lon
+    own = part // 2
+
+    def spread_rows(i, carry):
+        at = pl.ds(pl.multiple_of(i * block, 16), block)
+        row = i * block + lax.broadcasted_iota(jnp.int32, (block, 1), 0)
+        wanted = lax.rem(row, own) * nlat + lax.div(row, part)
+        column = lax.broadcasted_iota(jnp.int32, (block, leg_ref.shape[0]), 1)
+        pick = jnp.where(column == wanted, 1.0, 0.0).astype(bf16)
+        legs[at] = jnp.dot(pick, leg_ref[...], preferred_element_type=f32).astype(bf16)
+        return carry
+
+    lax.fori_loop(0, total // block, spread_rows, 0)
+
+    def grams(i, carry):
+        at = pl.ds(pl.multiple_of(i * block, 16), block)
+        product = lax.dot_general(
+            legs[at], legs[...], (((1,), (1,)), ((), ())), preferred_element_type=f32
+        )
+        gram[at] = (product * same[...]).astype(bf16)
+        return carry
+
+    lax.fori_loop(0, total // block, grams, 0)
+
     def await_out(step, carry):
         d = lax.rem(me + n - step, n)
         push(msg.at[d], recv.at[d], s_out.at[d], r_out.at[d], d, n_lon).wait_recv()
@@ -385,48 +399,82 @@
     lax.fori_loop(0, blocks, send_back, 0)
     back[me] = grid[me]
 
-    def await_back(step, carry):
-        d = lax.rem(me + n - step, n)
-        push(grid.at[d], back.at[d], s_back.at[d], r_back.at[d], d, n_lon).wait_recv()
-        return carry
-
-    lax.fori_loop(1, n, await_back, 0)
-
     relay_halo(1)
-    for a in range(own_rows):
-        wide = back[:, a * part : (a + 1) * part].astype(f32)
-        pack[a] = wide.reshape(pack.shape[1:]).astype(bf16)
-
-    def to_slab(t):
-        return push(pack, q_ref.at[lon], s_q.at[t], r_q.at[lon], lat * n_lon + t, n_lon)
-
-    keep = pltpu.make_async_copy(pack, q_ref.at[lon], own_sem)
+    span = n_lon * part
+
+    def group(i):
+        g = lax.rem(lat + 2 * n_lat - 1 - i, n_lat)
+        return g, pl.ds(pl.multiple_of(g * span, 16), span)
+
+    def to_slab(t, g, at):
+        return push(
+            pack.at[:, at],
+            q_ref.at[lon, :, at],
+            s_q.at[t, g],
+            r_q.at[lon, g],
+            lat * n_lon + t,
+            n_lon,
+        )
+
+    def got(t, g, at, slot):
+        dst = q_ref.at[t, :, at]
+        return push(dst, dst, s_q.at[t, g], r_q.at[slot, g], me, n_lon)
+
+    half = n_lon // 2
+    cross = lax.rem(lon + half, n_lon)
+    side = lax.rem(lon, half)
+    mate = lon - side + (half - 1 - side)
+    far = lax.rem(mate + half, n_lon)
+    paired = n_lon == 4
+    targets = (cross, mate) if paired else [lax.rem(lon + e, n_lon) for e in range(1, n_lon)]
+
+    def relay(g, at):
+        dst = q_ref.at[cross, :, at]
+        return push(dst, dst, s_q.at[far, g], r_q.at[n_lon, g], lat * n_lon + mate, n_lon)
+
+    def gather(i, carry):
+        g, at = group(i)
+        for e in range(n_lon):
+            d = g * n_lon + e
+
+            @pl.when(d != me)
+            def _():
+                push(grid.at[d], back.at[d], s_back.at[d], r_back.at[d], d, n_lon).wait_recv()
+
+        wide = back[pl.ds(g * n_lon, n_lon)].astype(f32)
+        for a in range(own_rows):
+            rows_a = wide[:, a * part : (a + 1) * part]
+            pack[a, at] = rows_a.reshape(span, wide.shape[2]).astype(bf16)
+        for t in targets:
+            to_slab(t, g, at).start()
+        return carry
+
+    lax.fori_loop(0, n_lat, gather, 0)
+    keep = pltpu.make_async_copy(pack, q_ref.at[lon], own_sem.at[0])
     keep.start()
-    half = n_lon // 2
-    side = lax.rem(lon, half)
-    cross = lax.rem(lon + half, n_lon)
-    if n_lon == 4:
-        mate = lon - side + (1 - side)
-        far = lax.rem(mate + half, n_lon)
-        to_slab(cross).start()
-        to_slab(mate).start()
-        push(pack, q_ref.at[cross], s_q.at[cross], r_q.at[cross], me, n_lon).wait_recv()
-        relay = push(
-            q_ref.at[cross], q_ref.at[cross], s_q.at[far], r_q.at[n_lon], lat * n_lon + mate, n_lon
-        )
-        relay.start()
-        push(pack, q_ref.at[mate], s_q.at[mate], r_q.at[mate], me, n_lon).wait_recv()
-        push(pack, q_ref.at[far], s_q.at[far], r_q.at[n_lon], me, n_lon).wait_recv()
-        to_slab(cross).wait_send()
-        to_slab(mate).wait_send()
-        relay.wait_send()
-    else:
-        for step in range(1, n_lon):
-            to_slab(lax.rem(lon + step, n_lon)).start()
-        for step in range(1, n_lon):
-            t = lax.rem(lon + step, n_lon)
-            push(pack, q_ref.at[t], s_q.at[t], r_q.at[t], me, n_lon).wait_recv()
-            to_slab(t).wait_send()
+
+    def hand_over(i, carry):
+        g, at = group(i)
+        got(cross, g, at, cross).wait_recv()
+        relay(g, at).start()
+        return carry
+
+    def finish(i, carry):
+        g, at = group(i)
+        for t in targets:
+            to_slab(t, g, at).wait_send()
+        if paired:
+            got(mate, g, at, mate).wait_recv()
+            got(far, g, at, n_lon).wait_recv()
+            relay(g, at).wait_send()
+        else:
+            for t in targets:
+                got(t, g, at, t).wait_recv()
+        return carry
+
+    if paired:
+        lax.fori_loop(0, n_lat, hand_over, 0)
+    lax.fori_loop(0, n_lat, finish, 0)
     keep.wait()
 
     for step in range(1, n_lon):
@@ -440,6 +488,12 @@
 
     lax.fori_loop(1, n, drain, 0)
 
+    own_block.wait()
+
+    @pl.when(jnp.logical_not(gets_other))
+    def _():
+        blank.wait()
+
     for c in range(2):
         to_mate(c).wait_send()
 
@@ -449,7 +503,7 @@
 
         @pl.when(gets_other)
         def _():
-            dst = halo_ref.at[odd, piece_of(c)]
+            dst = ext_ref.at[2 * odd, piece_of(c)]
             push(dst, dst, s_halo.at[2 + c], r_halo.at[2 + c], me, n_lon).wait_recv()
 
 
@@ -471,8 +525,8 @@
         functools.partial(spectral_kernel, n_lat, n_lon, own_rows),
         out_shape=(
             jax.ShapeDtypeStruct((n_lon, own_rows, q_rows, channels), bf16),
-            jax.ShapeDtypeStruct((2,) + flat_rim.shape, bf16),
-            jax.ShapeDtypeStruct((q_rows, lon_cols), bf16),
+            jax.ShapeDtypeStruct((3,) + flat_rim.shape, bf16),
+            jax.ShapeDtypeStruct((2, q_rows, lon_cols), bf16),
         ),
         in_specs=[vmem, anywhere, vmem, vmem],
         out_specs=(anywhere, anywhere, vmem),
@@ -485,10 +539,10 @@
         ]
         + [pltpu.VMEM((n, rows, channels), bf16)] * 4
         + [pltpu.VMEM((own_rows, q_rows, channels), bf16), pltpu.VMEM((total, leg.shape[1]), bf16)]
-        + [dma]
+        + [pltpu.VMEM(flat_rim.shape, bf16), dma((3,))]
         + [dma((n_lon,))] * 2
         + [dma((n,))] * 4
-        + [dma((n_lon,)), dma((n_lon + 1,))]
+        + [dma((n_lon, n_lat)), dma((n_lon + 1, n_lat))]
         + [dma((4,))] * 2,
         compiler_params=pltpu.CompilerParams(
             collective_id=1, has_side_effects=True, vmem_limit_bytes=52 * 2**20
@@ -536,6 +590,7 @@
     masked = jnp.where(mask[:, None, :], own_leg, jnp.zeros((), bf16))
     own_quad = lax.dynamic_slice_in_dim(quad_weight, lon_pos * own_rows, own_rows)
     rimmed = padded(field, (("lon", 1),), 1, True)
+    rimmed = jnp.pad(rimmed, ((0, 0), (0, -rimmed.shape[1] % 16), (0, 0)))
     if own % 4 == 0 and n_dev * own % 64 == 0 and own_rows * lon_cols % 16 == 0:
         shape = (n_dev, 2, own)
         factor = jnp.where(orders == 0, 1.0, 2.0)[:, None, :] / nlon
@@ -548,22 +603,11 @@
         leg = masked.reshape(-1, degrees)
         grid, halo, direct = spectral(field, rimmed, cols, leg, lax.axis_size("lat"), n_lon, own_rows)
         grid = grid.reshape(lat_rows, -1, channels)
-        pair = direct.reshape(n_dev, 2, own, lon_cols)
-        turned = jnp.stack([pair[:, 1], -pair[:, 0]], axis=1).reshape(-1, lon_cols)
         waves = [
             jnp.einsum("qj,aqc->ajc", piece, grid, preferred_element_type=f32).astype(bf16)
-            for piece in (direct, turned)
+            for piece in (direct[0], direct[1])
         ]
-        halo = halo.reshape(2, lat_rows, lon_cols + 2, channels)
-        zero = jnp.zeros((), bf16)
-        extended = jnp.concatenate(
-            [
-                jnp.where(lat_pos > 0, halo[0], zero),
-                rimmed,
-                jnp.where(lat_pos < lax.axis_size("lat") - 1, halo[1], zero),
-            ],
-            axis=0,
-        )
+        extended = halo.reshape(3 * lat_rows, -1, channels)
     else:
         column = jnp.arange(nlon, dtype=jnp.int32)
         phase = column[:, None] * flat_orders[None, :] % nlon

time: 182 us -> 162 us (0.89)
  local copies, waits for them, and re-layouts: 24.4 us -> 12.8 us
  Pallas kernels: 126 us -> 121 us
  other arithmetic: 10.4 us -> 6.89 us
    unnamed x34 -> x18, local copies, waits for them, and re-layouts: 7.78 us -> 2.3 us
    select_n x4 -> x0, local copies, waits for them, and re-layouts: 5.23 us -> none  [the longest x2 3.19 us: local(): jnp.where(lat_pos > 0, halo[0], zero)]
    select_n x1 -> x0, other arithmetic: 3.68 us -> none  [local(): jnp.where(lat_pos > 0, halo[0], zero)]
    reshape x3 -> x0, local copies, waits for them, and re-layouts: 3.23 us -> none  [the longest x1 1.65 us: local(): turned = jnp.stack([pair[:, 1], -pair[:, 0]], axis=1).reshape(-1, lon_cols)]
    pallas_call x1, Pallas kernels: 100 us -> 97 us  [spectral(): pl.pallas_call(functools.partial(spectral_kernel, n_lat, n_lon, own_rows)...]
    slice x1 -> x2, local copies, waits for them, and re-layouts: 0.9 us -> 3.49 us  [the longest x1 2.59 us: local(): window = extended[:, tap:tap + lon_cols]]
    pallas_call x1, Pallas kernels: 26.2 us -> 24.1 us  [reduce_all(): pl.pallas_call(functools.partial(reduce_kernel, n_lat, n_lon), out_shape=...]
  transfers between devices with their start and end apart: 2 -> 2, of which waited for: 0 -> 0; matrix products, arithmetic and copies ran while one was open for 3% -> 4% of each run, Pallas kernels for 0% -> 0%
where the time goes in v5:
time: 162 us
  Pallas kernels  121 us (75%)
  matrix products  17.1 us (11%)
  local copies, waits for them, and re-layouts  12.8 us (8%)
  other arithmetic  6.89 us (4%)
  between operations  2.33 us (1%)
  starting transfers between devices  1.83 us (1%)
    pallas_call x1, Pallas kernels, spectral(): pl.pallas_call(functools.partial(spectral_kernel, n_lat, n_lon, own_rows)...  97 us
    pallas_call x1, Pallas kernels, reduce_all(): pl.pallas_call(functools.partial(reduce_kernel, n_lat, n_lon), out_shape=...  24.1 us
    dot_general x2, matrix products, local(): jnp.einsum('qj,aqc->ajc', piece, grid, preferred_element_type=f32)  6.77 us
    dot_general x3, matrix products, local(): jnp.einsum('ab,boc->aoc', operator[tap], window, preferred_element_type=f32)  3.91 us
    dot_general x5, matrix products, outer_sum(): lax.dot_general(left, right, (((0,), (0,)), ((), ())), preferred_element_...  3.52 us
    convert_element_type x1, other arithmetic, local(): flat_grad = grad_pre.astype(bf16).reshape(-1, channels)  3.37 us
  transfers between devices with their start and end apart: 2, of which 0 were waited for; matrix products, arithmetic and copies ran while one was open for 4% of the time, Pallas kernels for 0%

profile of v5, /device:TPU:25, one launch (start us, length us, event | category | flops | bytes accessed | tf_op | source)
XLA Modules:
  0.0 162.0 jit_solution(17256498703396141233)
XLA Ops:
  0.7 0.9 fusion.82
  1.6 1.8 %collective-permute-start = (bf16[8,1,256]{2,1,0:T(2,128)(2,1)S(1)}, bf16[8,1,256]{2,1,0:T(2,128)(2,1)S(1)}, u32[]{:S(2)}, u32[]{:S(2)}) collective-permute-start(bf16[8,1,256]{2,1,0:T(2,128)(2,1)S(1)} %get-tuple-element.16), channel_id=1, source_target_pairs={{0,1},{1,2},{2,3},{3,0},{4,5},{5,6},{6,7},{7,4},{8,9},{9,10},{10,1... | collective-permute-start | bytes 12296 | tf_op jit(solution)/shard_map/ppermute | solution.py:23
  3.4 0.7 dynamic_slice.9
  4.1 0.6 fusion.84
  4.7 0.8 broadcast_in_dim_reshape.3
  7.2 0.7 broadcast_in_dim.29
  8.2 0.7 add_bitcast_fusion
  9.0 1.2 dynamic-slice_select_fusion
  10.7 1.6 fusion.29
  12.3 97.0 %shard_map.121 = (bf16[4,2,768,256]{3,2,1,0:T(8,128)(2,1)}, bf16[3,2944,256]{2,1,0:T(8,128)(2,1)}, bf16[2,768,360]{2,1,0:T(8,128)(2,1)}) custom-call(bf16[2880,256]{1,0:T(8,128)(2,1)} %bitcast.120, bf16[2944,256]{1,0:T(8,128)(2,1)} %bitcast.122, f32[768,4]{1,0:T(8,128)S(1)} %copy.38.cols_ref, bf16[768,384]{1,0:T(8,128)(2,1)S(1)} %bitcast.116), custom_call_target="tpu_custom_call" | custom-call | tf_op jit(solution)/shard_map/pallas_call | solution.py:524
  109.3 3.5 %convolution_convert_fusion = bf16[8,256,360]{1,2,0:T(8,128)(2,1)S(1)} fusion(bf16[8,768,256]{2,1,0:T(8,128)(2,1)} %bitcast.128, bf16[2,768,360]{2,1,0:T(8,128)(2,1)} %get-tuple-element.7), kind=kOutput, calls=%fused_computation.29 | convolution fusion | flops 1133199360 | bytes 5210112 | tf_op jit(solution)/shard_map/qj,aqc->ajc/dot_general | solution.py:607
  112.8 3.2 %convolution_convert_fusion.1 = bf16[8,256,360]{1,2,0:T(8,128)(2,1)S(1)} fusion(bf16[8,768,256]{2,1,0:T(8,128)(2,1)} %bitcast.129, bf16[2,768,360]{2,1,0:T(8,128)(2,1)S(1)} %copy-done.6), kind=kOutput, calls=%fused_computation.30 | convolution fusion | flops 1133199360 | bytes 5210112 | tf_op jit(solution)/shard_map/qj,aqc->ajc/dot_general | solution.py:607
  116.1 2.6 %fusion.81 = (bf16[24,360,256]{2,1,0:T(8,128)(2,1)S(1)}, bf16[24,360,256]{2,1,0:T(8,128)(2,1)S(1)}, bf16[24,360,256]{2,1,0:T(8,128)(2,1)S(1)}) fusion(bf16[24,368,256]{2,1,0:T(8,128)(2,1)S(1)} %bitcast.119), kind=kLoop, calls=%fused_computation.87 | loop fusion | bytes 26542080 | tf_op jit(solution)/shard_map/slice | solution.py:657
  118.7 1.3 fusion.19
  120.3 1.3 fusion.22
  121.9 1.3 fusion.25
  123.6 0.6 copy-done.5
  124.2 0.5 fusion.70
  124.8 0.6 convolution_add_fusion.3
  125.7 0.5 convolution_add_fusion.2
  126.3 0.5 convolution_add_fusion.1
  126.9 0.6 convolution_add_fusion
  127.5 0.8 copy-done.2
  128.7 3.4 %fusion.11 = (bf16[8,360,256]{2,1,0:T(8,128)(2,1)S(1)}, bf16[8,360,256]{2,1,0:T(8,128)(2,1)}) fusion(bf16[8,360,256]{2,1,0:T(8,128)(2,1)S(1)} %copy-done.3, f32[8,360,256]{2,1,0:T(8,128)S(1)} %bitcast.121, bf16[8,360,256]{2,1,0:T(8,128)(2,1)S(1)} %copy-done.2), kind=kLoop, calls=%fused_computation.20 | loop fusion | flops 18432000 | bytes 8847360 | tf_op jit(solution)/shard_map/convert_element_type | solution.py:671
  132.0 0.6 fusion.49
  132.7 0.6 fusion.43
  133.3 0.8 fusion.53
  134.1 0.8 fusion.55
  134.8 0.8 fusion.57
  135.8 24.1 %shard_map.122 = f32[2,16,80,128]{3,2,1,0:T(8,128)S(1)} custom-call(bf16[2,16,80,128]{3,2,1,0:T(8,128)(2,1)S(1)} %convert_element_type.69.x_ref), custom_call_target="tpu_custom_call" | custom-call | tf_op jit(solution)/shard_map/pallas_call | solution.py:149
  160.2 0.9 slice.86
  161.2 0.8 slice.85
  (44 shorter events, 3.6 us)
Async XLA Ops:
  0.6 8.2 %copy-start = (bf16[3,8,3,8]{3,1,2,0:T(8,128)(2,1)S(1)}, bf16[3,8,3,8]{3,1,2,0:T(8,128)(2,1)}, u32[]{:S(2)}) copy-start(bf16[3,8,3,8]{3,1,2,0:T(8,128)(2,1)} %param.16) | copy-start | bytes 3460
  0.6 10.0 %copy-start.1 = (bf16[8,360,256]{2,1,0:T(8,128)(2,1)S(1)}, bf16[8,360,256]{2,1,0:T(8,128)(2,1)}, u32[]{:S(2)}) copy-start(bf16[8,360,256]{2,1,0:T(8,128)(2,1)} %param.10) | copy-start | bytes 4423684
  1.6 9.1 %collective-permute-start = (bf16[8,1,256]{2,1,0:T(2,128)(2,1)S(1)}, bf16[8,1,256]{2,1,0:T(2,128)(2,1)S(1)}, u32[]{:S(2)}, u32[]{:S(2)}) collective-permute-start(bf16[8,1,256]{2,1,0:T(2,128)(2,1)S(1)} %get-tuple-element.16), channel_id=1, source_target_pairs={{0,1},{1,2},{2,3},{3,0},{4,5},{5,6},{6,7},{7,4},{8,9},{9,10},{10,1... | collective-permute-start | bytes 12296 | tf_op jit(solution)/shard_map/ppermute | solution.py:23
  3.4 7.3 %collective-permute-start.1 = (bf16[8,1,256]{2,1,0:T(2,128)(2,1)S(1)}, bf16[8,1,256]{2,1,0:T(2,128)(2,1)S(1)}, u32[]{:S(2)}, u32[]{:S(2)}) collective-permute-start(bf16[8,1,256]{2,1,0:T(2,128)(2,1)S(1)} %get-tuple-element.17), channel_id=1, source_target_pairs={{1,0},{2,1},{3,2},{0,3},{5,4},{6,5},{7,6},{4,7},{9,8},{10,9},{11,1... | collective-permute-start | bytes 12296 | tf_op jit(solution)/shard_map/ppermute | solution.py:24
  109.3 6.8 %slice-start = ((s8[4521984]{0:T(1024)(128)(4,1)}), s8[4194304]{0:T(1024)(128)(4,1)S(1)}, s32[]{:S(2)}) async-start(s8[4521984]{0:T(1024)(128)(4,1)} %bitcast.117), calls=%async_computation | async-start | bytes 8388608
  109.3 3.6 %copy-start.6 = (bf16[2,768,360]{2,1,0:T(8,128)(2,1)S(1)}, bf16[2,768,360]{2,1,0:T(8,128)(2,1)}, u32[]{:S(2)}) copy-start(bf16[2,768,360]{2,1,0:T(8,128)(2,1)} %get-tuple-element.7) | copy-start | bytes 3317764
  109.3 6.8 %slice-start.1 = ((s8[4521984]{0:T(1024)(128)(4,1)}), s8[327680]{0:T(1024)(128)(4,1)S(1)}, s32[]{:S(2)}) async-start(s8[4521984]{0:T(1024)(128)(4,1)} %bitcast.117), calls=%async_computation.1 | async-start | bytes 655360
  123.2 1.0 copy-start.5
  124.7 1.0 copy-start.4
  126.8 1.4 copy-start.2
  126.9 1.8 %copy-start.3 = (bf16[8,360,256]{2,1,0:T(8,128)(2,1)S(1)}, bf16[8,360,256]{2,1,0:T(8,128)(2,1)}, u32[]{:S(2)}) copy-start(bf16[8,360,256]{2,1,0:T(8,128)(2,1)} %param.11) | copy-start | bytes 4423684

commit v6 on v5

--- a/solution.py
+++ b/solution.py
@@ -8,6 +8,7 @@
 from jax.sharding import PartitionSpec as P
 
 MESH = pl.DeviceIdType.MESH
+PIECES = 4
 SINE = (2.7557319223985893e-6, -1.984126984126984e-4, 8.333333333333333e-3, -1 / 6, 1.0)
 
 BOTH = ("lat", "lon")
@@ -223,10 +224,11 @@
     has_other = jnp.logical_and(hand_to >= 0, hand_to < n_lat)
     from_other = lat - 2 * sign
     gets_other = jnp.logical_and(from_other >= 0, from_other < n_lat)
-    cut = rim_ref.shape[0] // 32 * 16
+    cut = rim_ref.shape[0] // (16 * PIECES) * 16
 
     def piece_of(c):
-        return pl.ds(cut, rim_ref.shape[0] - cut) if c else pl.ds(0, cut)
+        last = rim_ref.shape[0] - (PIECES - 1) * cut
+        return pl.ds(c * cut, cut if c < PIECES - 1 else last)
 
     def to_mate(c):
         at = piece_of(c)
@@ -249,8 +251,8 @@
         return push(
             ext_ref.at[2 - 2 * odd, at],
             ext_ref.at[2 * odd, at],
-            s_halo.at[2 + c],
-            r_halo.at[2 + c],
+            s_halo.at[PIECES + c],
+            r_halo.at[PIECES + c],
             hand_to * n_lon + lon,
             n_lon,
         )
@@ -261,6 +263,9 @@
         @pl.when(has_other)
         def _():
             hand_on(c).start()
+
+        if c < PIECES - 1:
+            to_mate(c + 1).start()
 
     def to_lon(t):
         src = field_ref.at[pl.ds(pl.multiple_of(t * band, 16), band)]
@@ -302,10 +307,12 @@
         tab_ref[1, at] = wave((j + (lon * lon_cols).astype(f32)) * order + (shift + nlon / 4.0))
         return carry
 
-    lax.fori_loop(0, table.shape[1] // chunk, tables, 0)
+    chunks = table.shape[1] // chunk
+    lax.fori_loop(0, chunks // 2, tables, 0)
+    relay_halo(0)
+    lax.fori_loop(chunks // 2, chunks, tables, 0)
     tab_ref[0] = table[lon]
-    relay_halo(0)
-    to_mate(1).start()
+    relay_halo(1)
 
     for step in range(n_lon):
         s = lax.rem(lon + step, n_lon)
@@ -373,6 +380,7 @@
         return carry
 
     lax.fori_loop(1, n, await_out, 0)
+    relay_halo(2)
 
     per = block // rows
     blocks = total // block
@@ -399,7 +407,6 @@
     lax.fori_loop(0, blocks, send_back, 0)
     back[me] = grid[me]
 
-    relay_halo(1)
     span = n_lon * part
 
     def group(i):
@@ -450,6 +457,7 @@
         return carry
 
     lax.fori_loop(0, n_lat, gather, 0)
+    relay_halo(3)
     keep = pltpu.make_async_copy(pack, q_ref.at[lon], own_sem.at[0])
     keep.start()
 
@@ -494,7 +502,7 @@
     def _():
         blank.wait()
 
-    for c in range(2):
+    for c in range(PIECES):
         to_mate(c).wait_send()
 
         @pl.when(has_other)
@@ -504,7 +512,7 @@
         @pl.when(gets_other)
         def _():
             dst = ext_ref.at[2 * odd, piece_of(c)]
-            push(dst, dst, s_halo.at[2 + c], r_halo.at[2 + c], me, n_lon).wait_recv()
+            push(dst, dst, s_halo.at[PIECES + c], r_halo.at[PIECES + c], me, n_lon).wait_recv()
 
 
 def spectral(field, rimmed, cols, leg, n_lat, n_lon, own_rows):
@@ -543,7 +551,7 @@
         + [dma((n_lon,))] * 2
         + [dma((n,))] * 4
         + [dma((n_lon, n_lat)), dma((n_lon + 1, n_lat))]
-        + [dma((4,))] * 2,
+        + [dma((2 * PIECES,))] * 2,
         compiler_params=pltpu.CompilerParams(
             collective_id=1, has_side_effects=True, vmem_limit_bytes=52 * 2**20
         ),

time: 162 us -> 160 us (0.988)
  Pallas kernels: 121 us -> 119 us
    pallas_call x1, Pallas kernels: 97 us -> 93.8 us  [spectral(): pl.pallas_call(functools.partial(spectral_kernel, n_lat, n_lon, own_rows)...]
where the time goes in v6:
time: 160 us
  Pallas kernels  119 us (74%)
  matrix products  17.1 us (11%)
  local copies, waits for them, and re-layouts  12.8 us (8%)
  other arithmetic  6.89 us (4%)
  between operations  2.33 us (1%)
  starting transfers between devices  1.83 us (1%)
    pallas_call x1, Pallas kernels, spectral(): pl.pallas_call(functools.partial(spectral_kernel, n_lat, n_lon, own_rows)...  93.8 us
    pallas_call x1, Pallas kernels, reduce_all(): pl.pallas_call(functools.partial(reduce_kernel, n_lat, n_lon), out_shape=...  25.3 us
    dot_general x2, matrix products, local(): jnp.einsum('qj,aqc->ajc', piece, grid, preferred_element_type=f32)  6.77 us
    dot_general x3, matrix products, local(): jnp.einsum('ab,boc->aoc', operator[tap], window, preferred_element_type=f32)  3.91 us
    dot_general x5, matrix products, outer_sum(): lax.dot_general(left, right, (((0,), (0,)), ((), ())), preferred_element_...  3.52 us
    convert_element_type x1, other arithmetic, local(): flat_grad = grad_pre.astype(bf16).reshape(-1, channels)  3.37 us
  transfers between devices with their start and end apart: 2, of which 0 were waited for; matrix products, arithmetic and copies ran while one was open for 4% of the time, Pallas kernels for 0%

profile of v6, /device:TPU:25, one launch (start us, length us, event | category | flops | bytes accessed | tf_op | source)
XLA Modules:
  0.0 160.1 jit_solution(5511874790784352578)
XLA Ops:
  0.7 0.9 fusion.82
  1.6 1.8 %collective-permute-start = (bf16[8,1,256]{2,1,0:T(2,128)(2,1)S(1)}, bf16[8,1,256]{2,1,0:T(2,128)(2,1)S(1)}, u32[]{:S(2)}, u32[]{:S(2)}) collective-permute-start(bf16[8,1,256]{2,1,0:T(2,128)(2,1)S(1)} %get-tuple-element.16), channel_id=1, source_target_pairs={{0,1},{1,2},{2,3},{3,0},{4,5},{5,6},{6,7},{7,4},{8,9},{9,10},{10,1... | collective-permute-start | bytes 12296 | tf_op jit(solution)/shard_map/ppermute | solution.py:24
  3.4 0.7 dynamic_slice.9
  4.1 0.6 fusion.84
  4.7 0.8 broadcast_in_dim_reshape.3
  7.2 0.7 broadcast_in_dim.29
  8.2 0.7 add_bitcast_fusion
  9.0 1.2 dynamic-slice_select_fusion
  10.7 1.6 fusion.29
  12.3 93.8 %shard_map.121 = (bf16[4,2,768,256]{3,2,1,0:T(8,128)(2,1)}, bf16[3,2944,256]{2,1,0:T(8,128)(2,1)}, bf16[2,768,360]{2,1,0:T(8,128)(2,1)}) custom-call(bf16[2880,256]{1,0:T(8,128)(2,1)} %bitcast.120, bf16[2944,256]{1,0:T(8,128)(2,1)} %bitcast.122, f32[768,4]{1,0:T(8,128)S(1)} %copy.38.cols_ref, bf16[768,384]{1,0:T(8,128)(2,1)S(1)} %bitcast.116), custom_call_target="tpu_custom_call" | custom-call | tf_op jit(solution)/shard_map/pallas_call | solution.py:532
  106.1 3.5 %convolution_convert_fusion = bf16[8,256,360]{1,2,0:T(8,128)(2,1)S(1)} fusion(bf16[8,768,256]{2,1,0:T(8,128)(2,1)} %bitcast.128, bf16[2,768,360]{2,1,0:T(8,128)(2,1)} %get-tuple-element.7), kind=kOutput, calls=%fused_computation.29 | convolution fusion | flops 1133199360 | bytes 5210112 | tf_op jit(solution)/shard_map/qj,aqc->ajc/dot_general | solution.py:615
  109.7 3.2 %convolution_convert_fusion.1 = bf16[8,256,360]{1,2,0:T(8,128)(2,1)S(1)} fusion(bf16[8,768,256]{2,1,0:T(8,128)(2,1)} %bitcast.129, bf16[2,768,360]{2,1,0:T(8,128)(2,1)S(1)} %copy-done.6), kind=kOutput, calls=%fused_computation.30 | convolution fusion | flops 1133199360 | bytes 5210112 | tf_op jit(solution)/shard_map/qj,aqc->ajc/dot_general | solution.py:615
  113.0 2.6 %fusion.81 = (bf16[24,360,256]{2,1,0:T(8,128)(2,1)S(1)}, bf16[24,360,256]{2,1,0:T(8,128)(2,1)S(1)}, bf16[24,360,256]{2,1,0:T(8,128)(2,1)S(1)}) fusion(bf16[24,368,256]{2,1,0:T(8,128)(2,1)S(1)} %bitcast.119), kind=kLoop, calls=%fused_computation.87 | loop fusion | bytes 26542080 | tf_op jit(solution)/shard_map/slice | solution.py:665
  115.5 1.3 fusion.19
  117.2 1.3 fusion.22
  118.8 1.3 fusion.25
  120.4 0.6 copy-done.5
  121.0 0.5 fusion.70
  121.6 0.6 convolution_add_fusion.3
  122.6 0.5 convolution_add_fusion.2
  123.1 0.5 convolution_add_fusion.1
  123.7 0.6 convolution_add_fusion
  124.3 0.8 copy-done.2
  125.5 3.4 %fusion.11 = (bf16[8,360,256]{2,1,0:T(8,128)(2,1)S(1)}, bf16[8,360,256]{2,1,0:T(8,128)(2,1)}) fusion(bf16[8,360,256]{2,1,0:T(8,128)(2,1)S(1)} %copy-done.3, f32[8,360,256]{2,1,0:T(8,128)S(1)} %bitcast.121, bf16[8,360,256]{2,1,0:T(8,128)(2,1)S(1)} %copy-done.2), kind=kLoop, calls=%fused_computation.20 | loop fusion | flops 18432000 | bytes 8847360 | tf_op jit(solution)/shard_map/convert_element_type | solution.py:679
  128.9 0.6 fusion.49
  129.5 0.6 fusion.43
  130.2 0.8 fusion.53
  130.9 0.8 fusion.55
  131.7 0.8 fusion.57
  132.6 25.3 %shard_map.122 = f32[2,16,80,128]{3,2,1,0:T(8,128)S(1)} custom-call(bf16[2,16,80,128]{3,2,1,0:T(8,128)(2,1)S(1)} %convert_element_type.69.x_ref), custom_call_target="tpu_custom_call" | custom-call | tf_op jit(solution)/shard_map/pallas_call | solution.py:150
  158.3 0.9 slice.86
  159.2 0.8 slice.85
  (44 shorter events, 3.6 us)
Async XLA Ops:
  0.6 8.2 %copy-start = (bf16[3,8,3,8]{3,1,2,0:T(8,128)(2,1)S(1)}, bf16[3,8,3,8]{3,1,2,0:T(8,128)(2,1)}, u32[]{:S(2)}) copy-start(bf16[3,8,3,8]{3,1,2,0:T(8,128)(2,1)} %param.16) | copy-start | bytes 3460
  0.6 10.0 %copy-start.1 = (bf16[8,360,256]{2,1,0:T(8,128)(2,1)S(1)}, bf16[8,360,256]{2,1,0:T(8,128)(2,1)}, u32[]{:S(2)}) copy-start(bf16[8,360,256]{2,1,0:T(8,128)(2,1)} %param.10) | copy-start | bytes 4423684
  1.6 9.1 %collective-permute-start = (bf16[8,1,256]{2,1,0:T(2,128)(2,1)S(1)}, bf16[8,1,256]{2,1,0:T(2,128)(2,1)S(1)}, u32[]{:S(2)}, u32[]{:S(2)}) collective-permute-start(bf16[8,1,256]{2,1,0:T(2,128)(2,1)S(1)} %get-tuple-element.16), channel_id=1, source_target_pairs={{0,1},{1,2},{2,3},{3,0},{4,5},{5,6},{6,7},{7,4},{8,9},{9,10},{10,1... | collective-permute-start | bytes 12296 | tf_op jit(solution)/shard_map/ppermute | solution.py:24
  3.4 7.3 %collective-permute-start.1 = (bf16[8,1,256]{2,1,0:T(2,128)(2,1)S(1)}, bf16[8,1,256]{2,1,0:T(2,128)(2,1)S(1)}, u32[]{:S(2)}, u32[]{:S(2)}) collective-permute-start(bf16[8,1,256]{2,1,0:T(2,128)(2,1)S(1)} %get-tuple-element.17), channel_id=1, source_target_pairs={{1,0},{2,1},{3,2},{0,3},{5,4},{6,5},{7,6},{4,7},{9,8},{10,9},{11,1... | collective-permute-start | bytes 12296 | tf_op jit(solution)/shard_map/ppermute | solution.py:25
  106.1 6.8 %slice-start = ((s8[4521984]{0:T(1024)(128)(4,1)}), s8[4194304]{0:T(1024)(128)(4,1)S(1)}, s32[]{:S(2)}) async-start(s8[4521984]{0:T(1024)(128)(4,1)} %bitcast.117), calls=%async_computation | async-start | bytes 8388608
  106.1 3.6 %copy-start.6 = (bf16[2,768,360]{2,1,0:T(8,128)(2,1)S(1)}, bf16[2,768,360]{2,1,0:T(8,128)(2,1)}, u32[]{:S(2)}) copy-start(bf16[2,768,360]{2,1,0:T(8,128)(2,1)} %get-tuple-element.7) | copy-start | bytes 3317764
  106.1 6.8 %slice-start.1 = ((s8[4521984]{0:T(1024)(128)(4,1)}), s8[327680]{0:T(1024)(128)(4,1)S(1)}, s32[]{:S(2)}) async-start(s8[4521984]{0:T(1024)(128)(4,1)} %bitcast.117), calls=%async_computation.1 | async-start | bytes 655360
  120.1 1.0 copy-start.5
  121.6 1.0 copy-start.4
  123.7 1.4 copy-start.2
  123.7 1.8 %copy-start.3 = (bf16[8,360,256]{2,1,0:T(8,128)(2,1)S(1)}, bf16[8,360,256]{2,1,0:T(8,128)(2,1)}, u32[]{:S(2)}) copy-start(bf16[8,360,256]{2,1,0:T(8,128)(2,1)} %param.11) | copy-start | bytes 4423684

commit v7 on v6

--- a/solution.py
+++ b/solution.py
@@ -312,7 +312,6 @@
     relay_halo(0)
     lax.fori_loop(chunks // 2, chunks, tables, 0)
     tab_ref[0] = table[lon]
-    relay_halo(1)
 
     for step in range(n_lon):
         s = lax.rem(lon + step, n_lon)
@@ -343,6 +342,7 @@
 
     lax.fori_loop(1, n, send_out, 0)
     recv[me] = message(me)
+    relay_halo(1)
 
     total = gram.shape[0]
     block = same.shape[0]

time: 160 us -> 158 us (0.988)
  Pallas kernels: 119 us -> 117 us
    pallas_call x1, Pallas kernels: 93.8 us -> 91.8 us  [spectral(): pl.pallas_call(functools.partial(spectral_kernel, n_lat, n_lon, own_rows)...]
where the time goes in v7:
time: 158 us
  Pallas kernels  117 us (74%)
  matrix products  17.1 us (11%)
  local copies, waits for them, and re-layouts  12.8 us (8%)
  other arithmetic  6.89 us (4%)
  between operations  2.33 us (1%)
  starting transfers between devices  1.83 us (1%)
    pallas_call x1, Pallas kernels, spectral(): pl.pallas_call(functools.partial(spectral_kernel, n_lat, n_lon, own_rows)...  91.8 us
    pallas_call x1, Pallas kernels, reduce_all(): pl.pallas_call(functools.partial(reduce_kernel, n_lat, n_lon), out_shape=...  25 us
    dot_general x2, matrix products, local(): jnp.einsum('qj,aqc->ajc', piece, grid, preferred_element_type=f32)  6.77 us
    dot_general x3, matrix products, local(): jnp.einsum('ab,boc->aoc', operator[tap], window, preferred_element_type=f32)  3.91 us
    dot_general x5, matrix products, outer_sum(): lax.dot_general(left, right, (((0,), (0,)), ((), ())), preferred_element_...  3.52 us
    convert_element_type x1, other arithmetic, local(): flat_grad = grad_pre.astype(bf16).reshape(-1, channels)  3.37 us
  transfers between devices with their start and end apart: 2, of which 0 were waited for; matrix products, arithmetic and copies ran while one was open for 4% of the time, Pallas kernels for 0%

profile of v7, /device:TPU:25, one launch (start us, length us, event | category | flops | bytes accessed | tf_op | source)
XLA Modules:
  0.0 157.8 jit_solution(10214391429282849656)
XLA Ops:
  0.7 0.9 fusion.82
  1.6 1.8 %collective-permute-start = (bf16[8,1,256]{2,1,0:T(2,128)(2,1)S(1)}, bf16[8,1,256]{2,1,0:T(2,128)(2,1)S(1)}, u32[]{:S(2)}, u32[]{:S(2)}) collective-permute-start(bf16[8,1,256]{2,1,0:T(2,128)(2,1)S(1)} %get-tuple-element.16), channel_id=1, source_target_pairs={{0,1},{1,2},{2,3},{3,0},{4,5},{5,6},{6,7},{7,4},{8,9},{9,10},{10,1... | collective-permute-start | bytes 12296 | tf_op jit(solution)/shard_map/ppermute | solution.py:24
  3.4 0.7 dynamic_slice.9
  4.1 0.6 fusion.84
  4.7 0.8 broadcast_in_dim_reshape.3
  7.2 0.7 broadcast_in_dim.29
  8.2 0.7 add_bitcast_fusion
  9.0 1.2 dynamic-slice_select_fusion
  10.7 1.6 %fusion.29 = bf16[8,368,256]{2,1,0:T(8,128)(2,1)} fusion(bf16[8,1,256]{2,1,0:T(2,128)(2,1)S(1)} %collective-permute-done.1, bf16[8,360,256]{2,1,0:T(8,128)(2,1)S(1)} %copy-done.1, bf16[8,1,256]{2,1,0:T(2,128)(2,1)S(1)} %collective-permute-done), kind=kLoop, calls=%fused_computation.35 | loop fusion | flops 7536640 | bytes 2990080 | tf_op jit(solution)/shard_map/concatenate | solution.py:26
  12.3 91.8 %shard_map.121 = (bf16[4,2,768,256]{3,2,1,0:T(8,128)(2,1)}, bf16[3,2944,256]{2,1,0:T(8,128)(2,1)}, bf16[2,768,360]{2,1,0:T(8,128)(2,1)}) custom-call(bf16[2880,256]{1,0:T(8,128)(2,1)} %bitcast.120, bf16[2944,256]{1,0:T(8,128)(2,1)} %bitcast.122, f32[768,4]{1,0:T(8,128)S(1)} %copy.38.cols_ref, bf16[768,384]{1,0:T(8,128)(2,1)S(1)} %bitcast.116), custom_call_target="tpu_custom_call" | custom-call | tf_op jit(solution)/shard_map/pallas_call | solution.py:532
  104.1 3.5 %convolution_convert_fusion = bf16[8,256,360]{1,2,0:T(8,128)(2,1)S(1)} fusion(bf16[8,768,256]{2,1,0:T(8,128)(2,1)} %bitcast.128, bf16[2,768,360]{2,1,0:T(8,128)(2,1)} %get-tuple-element.7), kind=kOutput, calls=%fused_computation.29 | convolution fusion | flops 1133199360 | bytes 5210112 | tf_op jit(solution)/shard_map/qj,aqc->ajc/dot_general | solution.py:615
  107.7 3.2 %convolution_convert_fusion.1 = bf16[8,256,360]{1,2,0:T(8,128)(2,1)S(1)} fusion(bf16[8,768,256]{2,1,0:T(8,128)(2,1)} %bitcast.129, bf16[2,768,360]{2,1,0:T(8,128)(2,1)S(1)} %copy-done.6), kind=kOutput, calls=%fused_computation.30 | convolution fusion | flops 1133199360 | bytes 5210112 | tf_op jit(solution)/shard_map/qj,aqc->ajc/dot_general | solution.py:615
  110.9 2.6 %fusion.81 = (bf16[24,360,256]{2,1,0:T(8,128)(2,1)S(1)}, bf16[24,360,256]{2,1,0:T(8,128)(2,1)S(1)}, bf16[24,360,256]{2,1,0:T(8,128)(2,1)S(1)}) fusion(bf16[24,368,256]{2,1,0:T(8,128)(2,1)S(1)} %bitcast.119), kind=kLoop, calls=%fused_computation.87 | loop fusion | bytes 26542080 | tf_op jit(solution)/shard_map/slice | solution.py:665
  113.5 1.3 fusion.19
  115.2 1.3 fusion.22
  116.8 1.3 fusion.25
  118.4 0.6 copy-done.5
  119.0 0.5 fusion.70
  119.6 0.6 convolution_add_fusion.3
  120.6 0.5 convolution_add_fusion.2
  121.1 0.5 convolution_add_fusion.1
  121.7 0.6 convolution_add_fusion
  122.3 0.8 copy-done.2
  123.5 3.4 %fusion.11 = (bf16[8,360,256]{2,1,0:T(8,128)(2,1)S(1)}, bf16[8,360,256]{2,1,0:T(8,128)(2,1)}) fusion(bf16[8,360,256]{2,1,0:T(8,128)(2,1)S(1)} %copy-done.3, f32[8,360,256]{2,1,0:T(8,128)S(1)} %bitcast.121, bf16[8,360,256]{2,1,0:T(8,128)(2,1)S(1)} %copy-done.2), kind=kLoop, calls=%fused_computation.20 | loop fusion | flops 18432000 | bytes 8847360 | tf_op jit(solution)/shard_map/convert_element_type | solution.py:679
  126.9 0.6 fusion.49
  127.5 0.6 fusion.43
  128.2 0.8 fusion.53
  128.9 0.8 fusion.55
  129.7 0.8 fusion.57
  130.6 25.0 %shard_map.122 = f32[2,16,80,128]{3,2,1,0:T(8,128)S(1)} custom-call(bf16[2,16,80,128]{3,2,1,0:T(8,128)(2,1)S(1)} %convert_element_type.69.x_ref), custom_call_target="tpu_custom_call" | custom-call | tf_op jit(solution)/shard_map/pallas_call | solution.py:150
  156.0 0.9 slice.86
  156.9 0.8 slice.85
  (44 shorter events, 3.6 us)
Async XLA Ops:
  0.6 8.2 %copy-start = (bf16[3,8,3,8]{3,1,2,0:T(8,128)(2,1)S(1)}, bf16[3,8,3,8]{3,1,2,0:T(8,128)(2,1)}, u32[]{:S(2)}) copy-start(bf16[3,8,3,8]{3,1,2,0:T(8,128)(2,1)} %param.16) | copy-start | bytes 3460
  0.6 10.0 %copy-start.1 = (bf16[8,360,256]{2,1,0:T(8,128)(2,1)S(1)}, bf16[8,360,256]{2,1,0:T(8,128)(2,1)}, u32[]{:S(2)}) copy-start(bf16[8,360,256]{2,1,0:T(8,128)(2,1)} %param.10) | copy-start | bytes 4423684
  1.6 9.1 %collective-permute-start = (bf16[8,1,256]{2,1,0:T(2,128)(2,1)S(1)}, bf16[8,1,256]{2,1,0:T(2,128)(2,1)S(1)}, u32[]{:S(2)}, u32[]{:S(2)}) collective-permute-start(bf16[8,1,256]{2,1,0:T(2,128)(2,1)S(1)} %get-tuple-element.16), channel_id=1, source_target_pairs={{0,1},{1,2},{2,3},{3,0},{4,5},{5,6},{6,7},{7,4},{8,9},{9,10},{10,1... | collective-permute-start | bytes 12296 | tf_op jit(solution)/shard_map/ppermute | solution.py:24
  3.4 7.3 %collective-permute-start.1 = (bf16[8,1,256]{2,1,0:T(2,128)(2,1)S(1)}, bf16[8,1,256]{2,1,0:T(2,128)(2,1)S(1)}, u32[]{:S(2)}, u32[]{:S(2)}) collective-permute-start(bf16[8,1,256]{2,1,0:T(2,128)(2,1)S(1)} %get-tuple-element.17), channel_id=1, source_target_pairs={{1,0},{2,1},{3,2},{0,3},{5,4},{6,5},{7,6},{4,7},{9,8},{10,9},{11,1... | collective-permute-start | bytes 12296 | tf_op jit(solution)/shard_map/ppermute | solution.py:25
  104.1 6.8 %slice-start = ((s8[4521984]{0:T(1024)(128)(4,1)}), s8[4194304]{0:T(1024)(128)(4,1)S(1)}, s32[]{:S(2)}) async-start(s8[4521984]{0:T(1024)(128)(4,1)} %bitcast.117), calls=%async_computation | async-start | bytes 8388608
  104.1 3.6 %copy-start.6 = (bf16[2,768,360]{2,1,0:T(8,128)(2,1)S(1)}, bf16[2,768,360]{2,1,0:T(8,128)(2,1)}, u32[]{:S(2)}) copy-start(bf16[2,768,360]{2,1,0:T(8,128)(2,1)} %get-tuple-element.7) | copy-start | bytes 3317764
  104.1 6.8 %slice-start.1 = ((s8[4521984]{0:T(1024)(128)(4,1)}), s8[327680]{0:T(1024)(128)(4,1)S(1)}, s32[]{:S(2)}) async-start(s8[4521984]{0:T(1024)(128)(4,1)} %bitcast.117), calls=%async_computation.1 | async-start | bytes 655360
  118.1 1.0 copy-start.5
  119.6 1.0 copy-start.4
  121.7 1.4 copy-start.2
  121.7 1.8 %copy-start.3 = (bf16[8,360,256]{2,1,0:T(8,128)(2,1)S(1)}, bf16[8,360,256]{2,1,0:T(8,128)(2,1)}, u32[]{:S(2)}) copy-start(bf16[8,360,256]{2,1,0:T(8,128)(2,1)} %param.11) | copy-start | bytes 4423684
